TPU v7x, 512 devices: a whole 4x8x8 slice. The times are simulated.
512 devices in a mesh: dp: 64 (over x, z, core), tensor: 8 (over y).
Axes of the slice: x: 4, y: 8, z: 8, core: 2. Of those that a mesh axis runs over, the one named last changes fastest.
Arguments:
- grads: float32 [64, 4096, 512], P('dp', 'tensor'), may hold values from -80 to 80
- signs: int32 [4096, 512], P('tensor'), may hold values from -1 to 1, as said below
- dither: int32 [64, 4096, 512], P('dp', 'tensor'), may hold values from 0 to 4095
Outputs:
- mean_grad: float32 [4096, 512], P('tensor')
- quant_step: float32 [], replicated
Inputs may be any that keep to these rules, and one draw needn't show every extreme that they name: `signs`: every entry is -1 or 1.
All inputs are finite; a program needn't handle non-finite values. Where the computation divides by a largest or mean magnitude, that divisor is 1e-20 or more.
Results may differ from a plain program's by a relative error of at most 0.0008.
Values sent between devices are 32-bit elements; how exact they have to be, the bound alone decides.
No kernel may reach another device: no remote copies, remote signals or barrier semaphores. Data moves between devices by JAX's collectives and lax.ppermute only.
A program may use at most 64 MiB of HBM per device.

v0:
```python
import math

import jax
import jax.numpy as jnp
from jax import lax
from jax.sharding import PartitionSpec as P


def hadamard(length):
    indices = jnp.arange(length, dtype=jnp.int32)
    common_bits = jnp.bitwise_and(indices[:, None], indices[None, :])
    parity = jnp.zeros((length, length), jnp.int32)
    for position in range(length.bit_length()):
        parity = parity + jnp.bitwise_and(jnp.right_shift(common_bits, position), 1)
    return (1 - 2 * (parity % 2)).astype(jnp.float32) / math.sqrt(length)


def rotate(values, matrix):
    return jnp.dot(
        values, matrix, precision=lax.Precision.HIGHEST, preferred_element_type=jnp.float32
    )


def shards(grads, signs, dither):
    length = grads.shape[2]
    matrix = hadamard(length)
    replicas = lax.axis_size("dp")
    sign_vals = signs.astype(jnp.float32)
    rotated = rotate(grads[0] * sign_vals, matrix)
    peak = lax.pmax(jnp.max(jnp.abs(rotated)), ("dp", "tensor"))
    scale = 127.0 / peak
    codes = jnp.floor(rotated * scale + dither[0].astype(jnp.float32) * 2.0 ** (-12))
    quant_step = peak / 127.0
    factor = quant_step / replicas
    owned = lax.psum_scatter(codes, "dp", scatter_dimension=0, tiled=True)
    total = lax.all_gather(owned, "dp", axis=0, tiled=True)
    mean_grad = sign_vals * (rotate(total, matrix) * factor)
    return (mean_grad, quant_step)


def solution(mesh):
    return jax.shard_map(
        shards,
        mesh=mesh,
        in_specs=(P("dp", "tensor", None), P("tensor", None), P("dp", "tensor", None)),
        out_specs=(P("tensor", None), P()),
        check_vma=False,
    )
```

profile of v0, /device:TPU:1, one launch (start us, length us, event | category | flops | bytes accessed | tf_op | source)
XLA Modules:
  0.0 361.4 jit_solution(1560864314207268443)
XLA Ops:
  7.2 0.0 copy-start
  7.2 0.0 reduce-scatter.2.cloned.1.call-start
  7.2 5.8 %abs_reduce_fusion = (f32[]{:T(128)}, f32[512,512]{1,0:T(8,128)S(1)}) fusion(f32[1,512,512]{2,1,0:T(8,128)} %param.3, s32[512,512]{1,0:T(8,128)} %param.4), kind=kOutput, calls=%fused_computation.14 | convolution fusion | flops 1623457792 | bytes 3145732 | tf_op jit(solution)/shard_map/dot_general | solution.py:19
  13.0 106.1 %pmax.7 = f32[]{:T(128)} all-reduce(f32[]{:T(128)} %get-tuple-element.2), channel_id=1, replica_groups=mesh['dp'=64,'tensor'=8] {'dp','tensor'}, use_global_device_ids=true, to_apply=%region_1.2 | all-reduce | flops 1 | bytes 8 | tf_op jit(solution)/shard_map/pmax | solution.py:30
  119.8 0.0 copy-done
  119.8 1.2 fusion.6
  121.0 0.0 copy-start.1
  121.0 0.0 reduce-scatter.2.cloned.1.call-update
  121.0 0.0 all-gather.2.cloned.1.call-start
  121.1 137.4 %reduce-scatter.2.cloned.1.call-done = f32[8,512]{1,0:T(8,128)} async-done(((f32[512,512]{1,0:T(8,128)}), f32[8,512]{1,0:T(8,128)}) %reduce-scatter.2.cloned.1.call-update) | async-done | bytes 16400 | tf_op jit(solution)/shard_map/reduce_scatter | solution.py:35
  258.5 0.0 all-gather.2.cloned.1.call-update
  259.8 88.0 %all-gather.2.cloned.1.call-done = f32[512,512]{1,0:T(8,128)} async-done(((f32[8,512]{1,0:T(8,128)}), f32[512,512]{1,0:T(8,128)}) %all-gather.2.cloned.1.call-update) | async-done | bytes 1048592 | tf_op jit(solution)/shard_map/all_gather | solution.py:36
  347.8 0.0 copy-done.1
  347.8 5.7 %fusion = f32[512,512]{1,0:T(8,128)} fusion(f32[512,512]{1,0:T(8,128)} %all-gather.2.cloned.1.call-done, s32[512,512]{1,0:T(8,128)S(1)} %copy-done.1, f32[]{:T(128)S(6)} %div.20), kind=kOutput, calls=%fused_computation.4 | convolution fusion | flops 1623195648 | bytes 3145732 | tf_op jit(solution)/shard_map/dot_general | solution.py:19
Async XLA Ops:
  7.2 112.6 %copy-start = (s32[1,512,512]{2,1,0:T(8,128)S(1)}, s32[1,512,512]{2,1,0:T(8,128)}, u32[]{:S(2)}) copy-start(s32[1,512,512]{2,1,0:T(8,128)} %param.5) | copy-start | bytes 3145732
  7.2 251.3 %reduce-scatter.2.cloned.1.call-start = ((), (), s32[]{:S(2)}) async-start(), calls=%async_computation.1 | async-start | bytes 1064960 | tf_op jit(solution)/shard_map/reduce_scatter | solution.py:35
  121.0 226.8 %copy-start.1 = (s32[512,512]{1,0:T(8,128)S(1)}, s32[512,512]{1,0:T(8,128)}, u32[]{:S(2)}) copy-start(s32[512,512]{1,0:T(8,128)} %param.4) | copy-start | bytes 3145732
  121.0 226.7 %all-gather.2.cloned.1.call-start = ((), (), s32[]{:S(2)}) async-start(), calls=%async_computation.2 | async-start | bytes 1064960 | tf_op jit(solution)/shard_map/all_gather | solution.py:36
Sparse Core Ops, SparseCore 0:
  121.1 137.3 reduce-scatter.1
  261.8 85.8 all-gather.1
where the time goes:
time: 362 us; the launch traced here: 361 us
  waiting for transfers between devices  225 us (62%)
  blocking collectives  106 us (29%)
  between operations  17.2 us (5%)
  matrix products  11.4 us (3%)
    reduce_scatter x1, waiting for transfers between devices, shards(): owned = lax.psum_scatter(codes, 'dp', scatter_dimension=0, tiled=True)  137 us
    pmax x1, blocking collectives, shards(): peak = lax.pmax(jnp.max(jnp.abs(rotated)), ('dp', 'tensor'))  106 us
    all_gather x1, waiting for transfers between devices, shards(): total = lax.all_gather(owned, 'dp', axis=0, tiled=True)  88 us
    dot_general x2, matrix products, rotate(): jnp.dot(values, matrix, precision=lax.Precision.HIGHEST, preferred_elemen...  11.4 us
  transfers between devices with their start and end apart: 2, of which 2 were waited for; matrix products, arithmetic and copies ran while one was open for 0% of the time, Pallas kernels for 0%

commit v1 on v0

v1 whole, which is shorter than its diff:
```python
import math

import jax
import jax.numpy as jnp
import numpy as np
from jax import lax
from jax.experimental import pallas as pl
from jax.experimental.pallas import tpu as pltpu
from jax.sharding import Mesh, PartitionSpec as P

Z, CORES = 8, 2
CHIPS = ("x", "z")
STRIPE = 128


def signs_matrix(length):
    matrix = np.ones((1, 1), np.float32)
    while matrix.shape[0] < length:
        matrix = np.block([[matrix, matrix], [matrix, -matrix]])
    return jnp.asarray(matrix, jnp.bfloat16)


def butterfly(values):
    half = values.shape[1] // 2
    left, right = values[:, :half], values[:, half:]
    return jnp.concatenate([left + right, left - right], axis=0)


def parts_of(values, count):
    parts = []
    for _ in range(count):
        part = values.astype(jnp.bfloat16)
        parts.append(part)
        values = values - part.astype(jnp.float32)
    return parts


def transform(values, matrix, count):
    rows, length = values.shape
    parts = parts_of(butterfly(values), count)
    out = jnp.dot(parts[-1], matrix, preferred_element_type=jnp.float32)
    for part in parts[-2::-1]:
        out = out + jnp.dot(part, matrix, preferred_element_type=jnp.float32)
    out = out * (1.0 / math.sqrt(length))
    return jnp.concatenate([out[:rows], out[rows:]], axis=1)


def rotate_kernel(place, grads, signs, dither, matrix, own, send, top):
    step = pl.program_id(0)
    steps = pl.num_programs(0) // 2
    half = own.shape[0]
    rotated = transform(grads[...] * signs[...].astype(jnp.float32), matrix[...], 3)
    highest = jnp.max(jnp.abs(rotated).reshape(STRIPE // 8, 8, -1), axis=0)

    @pl.when(step == 0)
    def _():
        top[...] = highest

    @pl.when(step > 0)
    def _():
        top[...] = jnp.maximum(top[...], highest)

    @pl.when(step < steps)
    def _():
        at = pl.multiple_of(step * STRIPE, STRIPE)
        send[pl.ds(at, STRIPE), :] = rotated
        send[pl.ds(pl.multiple_of(half + at, STRIPE), STRIPE), :] = dither[...].astype(jnp.float32)

    @pl.when(step >= steps)
    def _():
        own[pl.ds(pl.multiple_of((step - steps) * STRIPE, STRIPE), STRIPE), :] = rotated

    @pl.when(step == 2 * steps - 1)
    def _():
        send[2 * half :, :] = top[...]


def rotate(place, grads, signs, dither, matrix):
    rows, length = grads.shape
    half = rows // 2
    steps = half // STRIPE

    def block(i, place):
        core = jnp.where(i < steps, 1 - place[0], place[0])
        return (core * steps + lax.rem(i, steps), 0)

    def others(i, place):
        return ((1 - place[0]) * steps + jnp.minimum(i, steps - 1), 0)

    whole = lambda i, place: (0, 0)
    return pl.pallas_call(
        rotate_kernel,
        grid_spec=pltpu.PrefetchScalarGridSpec(
            num_scalar_prefetch=1,
            grid=(2 * steps,),
            in_specs=[
                pl.BlockSpec((STRIPE, length), block),
                pl.BlockSpec((STRIPE, length), block),
                pl.BlockSpec((STRIPE, length), others),
                pl.BlockSpec(matrix.shape, whole),
            ],
            out_specs=[
                pl.BlockSpec((half, length), whole),
                pl.BlockSpec((rows + 8, length), whole),
            ],
            scratch_shapes=[pltpu.VMEM((8, length), jnp.float32)],
        ),
        out_shape=[
            jax.ShapeDtypeStruct((half, length), jnp.float32),
            jax.ShapeDtypeStruct((rows + 8, length), jnp.float32),
        ],
        compiler_params=pltpu.CompilerParams(vmem_limit_bytes=24 * 2**20),
        name="rotate",
    )(place, grads, signs, dither, matrix)


def chip_top_kernel(mine, theirs, out):
    out[...] = jnp.full(out.shape, jnp.max(jnp.maximum(mine[...], theirs[...])), jnp.float32)


def chip_top(sent, received, peers):
    rows, length = sent.shape
    last = pl.BlockSpec((8, length), lambda i: (rows // 8 - 1, 0))
    return pl.pallas_call(
        chip_top_kernel,
        grid=(1,),
        in_specs=[last, last],
        out_specs=pl.BlockSpec((peers, 128), lambda i: (0, 0)),
        out_shape=jax.ShapeDtypeStruct((peers, 128), jnp.float32),
        name="chip_top",
    )(sent, received)


def codes_kernel(place, tops, own, dither, other, other_dither, codes, quant_step):
    top = jnp.max(tops[...], axis=0, keepdims=True)
    scale = jnp.concatenate([127.0 / top] * (own.shape[1] // 128), axis=1)
    first = jnp.floor(own[...] * scale + dither[...].astype(jnp.float32) * 2.0 ** (-12))
    second = jnp.floor(other[...] * scale + other_dither[...] * 2.0 ** (-12))
    codes[...] = first + second
    quant_step[0, 0] = jnp.max(top / 127.0)


def chip_codes(place, tops, own, dither, received):
    half, length = own.shape
    steps = half // STRIPE
    stripe = lambda index: pl.BlockSpec((STRIPE, length), index)
    return pl.pallas_call(
        codes_kernel,
        grid_spec=pltpu.PrefetchScalarGridSpec(
            num_scalar_prefetch=1,
            grid=(steps,),
            in_specs=[
                pl.BlockSpec(tops.shape, lambda i, place: (0, 0)),
                stripe(lambda i, place: (i, 0)),
                stripe(lambda i, place: (place[0] * steps + i, 0)),
                stripe(lambda i, place: (i, 0)),
                stripe(lambda i, place: (steps + i, 0)),
            ],
            out_specs=[
                stripe(lambda i, place: (i, 0)),
                pl.BlockSpec(memory_space=pltpu.SMEM),
            ],
        ),
        out_shape=[
            jax.ShapeDtypeStruct((half, length), jnp.float32),
            jax.ShapeDtypeStruct((1, 1), jnp.float32),
        ],
        compiler_params=pltpu.CompilerParams(vmem_limit_bytes=24 * 2**20),
        name="chip_codes",
    )(place, tops, own, dither, received, received)


def mean_kernel(replicas, place, codes, signs, matrix, quant_step, out):
    total = jnp.sum(codes[...], axis=0)
    back = transform(total, matrix[...], 2)
    mean = signs[...].astype(jnp.float32) * (back * (quant_step[0, 0] * (1.0 / replicas)))
    out[...] = jnp.broadcast_to(mean[None], out.shape)


def owned_mean(replicas, place, codes, signs, matrix, quant_step):
    peers, rows, length = codes.shape
    whole = lambda i, place: (0, 0, 0)
    return pl.pallas_call(
        lambda *refs: mean_kernel(replicas, *refs),
        grid_spec=pltpu.PrefetchScalarGridSpec(
            num_scalar_prefetch=1,
            grid=(1,),
            in_specs=[
                pl.BlockSpec(codes.shape, whole),
                pl.BlockSpec((rows, length), lambda i, place: (place[1], 0)),
                pl.BlockSpec(matrix.shape, lambda i, place: (0, 0)),
                pl.BlockSpec(memory_space=pltpu.SMEM),
            ],
            out_specs=pl.BlockSpec(codes.shape, whole),
        ),
        out_shape=jax.ShapeDtypeStruct(codes.shape, jnp.float32),
        name="owned_mean",
    )(place, codes, signs, matrix, quant_step)


def shards(grads, signs, dither):
    _, rows, length = grads.shape
    chips = lax.axis_size(CHIPS)
    peers = lax.axis_size(CHIPS + ("tensor",))
    core = lax.axis_index("core")
    place = jnp.stack([core, core * chips + lax.axis_index(CHIPS)]).astype(jnp.int32)
    swap = [(0, 1), (1, 0)]
    matrix = signs_matrix(length // 2)

    own, send = rotate(place, grads[0], signs, dither[0], matrix)
    received = lax.ppermute(send, "core", swap)

    tops = chip_top(send, received, peers).reshape(peers, 1, 128)
    tops = lax.all_to_all(tops, CHIPS + ("tensor",), 0, 0).reshape(peers, 128)

    codes, quant_step = chip_codes(place, tops, own, dither[0], received)
    codes = codes.reshape(chips, rows // 2 // chips, length)
    codes = lax.all_to_all(codes, CHIPS, 0, 0)

    mean = owned_mean(CORES * chips, place, codes, signs, matrix, quant_step)
    mean = lax.all_to_all(mean, CHIPS, 0, 0).reshape(rows // 2, length)

    other = lax.ppermute(mean, "core", swap)
    low = core == 0
    mean_grad = jnp.concatenate([jnp.where(low, mean, other), jnp.where(low, other, mean)], axis=0)
    return (mean_grad, quant_step.reshape(()))


def solution(mesh):
    tensor = mesh.shape["tensor"]
    devices = mesh.devices.reshape(-1, Z, CORES, tensor)
    fine = Mesh(devices, ("x", "z", "core", "tensor"))
    dp = ("x", "z", "core")
    return jax.shard_map(
        shards,
        mesh=fine,
        in_specs=(P(dp, "tensor", None), P("tensor", None), P(dp, "tensor", None)),
        out_specs=(P("tensor", None), P()),
        check_vma=False,
    )
```

time: 362 us -> 105 us (0.29)
  waiting for transfers between devices: 225 us -> 3.8 us
  blocking collectives: 106 us -> 65.9 us
  between operations: 17.2 us -> 0.71 us
  starting transfers between devices: 0.08 us -> 16.1 us
  matrix products: 11.4 us -> 0 us
  local copies, waits for them, and re-layouts: 0.01 us -> 8.63 us
  Pallas kernels: 0 us -> 8.19 us
    reduce_scatter x1 -> x0, waiting for transfers between devices: 137 us -> none  [shards(): owned = lax.psum_scatter(codes, 'dp', scatter_dimension=0, tiled=True)]
    pmax x1 -> x0, blocking collectives: 106 us -> none  [shards(): peak = lax.pmax(jnp.max(jnp.abs(rotated)), ('dp', 'tensor'))]
    all_gather x1 -> x0, waiting for transfers between devices: 88 us -> none  [shards(): total = lax.all_gather(owned, 'dp', axis=0, tiled=True)]
    all_to_all x0 -> x3, blocking collectives: none -> 65.9 us  [the longest x1 28.8 us: shards(): tops = lax.all_to_all(tops, CHIPS + ('tensor',), 0, 0).reshape(peers, 128)]
    ppermute x0 -> x2, starting transfers between devices: none -> 16.1 us  [the longest x1 8.91 us: shards(): received = lax.ppermute(send, 'core', swap)]
    dot_general x2 -> x0, matrix products: 11.4 us -> none  [rotate(): jnp.dot(values, matrix, precision=lax.Precision.HIGHEST, preferred_elemen...]
    unnamed x4 -> x22, local copies, waits for them, and re-layouts: 0.01 us -> 8.63 us
    pallas_call x0 -> x4, Pallas kernels: none -> 8.19 us  [the longest x1 3.41 us: owned_mean(): pl.pallas_call(lambda *refs: mean_kernel(replicas, *refs), grid_spec=pltp...]
where the time goes in v1:
time: 105 us
  blocking collectives  65.9 us (63%)
  starting transfers between devices  16.1 us (15%)
  local copies, waits for them, and re-layouts  8.63 us (8%)
  Pallas kernels  8.19 us (8%)
  waiting for transfers between devices  3.8 us (4%)
  other arithmetic  1.23 us (1%)
    all_to_all x1, blocking collectives, shards(): tops = lax.all_to_all(tops, CHIPS + ('tensor',), 0, 0).reshape(peers, 128)  28.8 us
    all_to_all x1, blocking collectives, shards(): mean = lax.all_to_all(mean, CHIPS, 0, 0).reshape(rows // 2, length)  20.2 us
    all_to_all x1, blocking collectives, shards(): codes = lax.all_to_all(codes, CHIPS, 0, 0)  16.8 us
    ppermute x1, starting transfers between devices, shards(): received = lax.ppermute(send, 'core', swap)  8.91 us
    unnamed x22, local copies, waits for them, and re-layouts  8.63 us
    ppermute x1, starting transfers between devices, shards(): other = lax.ppermute(mean, 'core', swap)  7.19 us
    pallas_call x1, Pallas kernels, owned_mean(): pl.pallas_call(lambda *refs: mean_kernel(replicas, *refs), grid_spec=pltp...  3.41 us
    ppermute x1, waiting for transfers between devices, shards(): received = lax.ppermute(send, 'core', swap)  2.29 us
  transfers between devices with their start and end apart: 2, of which 2 were waited for; matrix products, arithmetic and copies ran while one was open for 0% of the time, Pallas kernels for 0%

profile of v1, /device:TPU:1, one launch (start us, length us, event | category | flops | bytes accessed | tf_op | source)
XLA Modules:
  0.0 104.5 jit_solution(15033144016597887776)
XLA Ops:
  0.6 0.1 pad_add_fusion.place.refs_0_
  0.7 1.2 %copy-done.2 = s32[512,512]{1,0:T(8,128)S(1)} copy-done((s32[512,512]{1,0:T(8,128)S(1)}, s32[512,512]{1,0:T(8,128)}, u32[]{:S(2)}) %copy-start.2) | copy-done | bytes 1048600
  1.9 1.2 %copy-done.3 = s32[1,512,512]{2,1,0:T(8,128)S(1)} copy-done((s32[1,512,512]{2,1,0:T(8,128)S(1)}, s32[1,512,512]{2,1,0:T(8,128)}, u32[]{:S(2)}) %copy-start.3) | copy-done | bytes 1048600
  3.2 1.2 %copy-done.6 = f32[1,512,512]{2,1,0:T(8,128)S(1)} copy-done((f32[1,512,512]{2,1,0:T(8,128)S(1)}, f32[1,512,512]{2,1,0:T(8,128)}, u32[]{:S(2)}) %copy-start.6) | copy-done | bytes 1048600
  4.4 0.9 copy-done.7
  5.3 1.9 %rotate.1 = (f32[256,512]{1,0:T(8,128)S(1)}, f32[520,512]{1,0:T(8,128)S(1)}) custom-call(s32[2]{0:T(128)S(1)} %pad_add_fusion.place.refs_0_, f32[512,512]{1,0:T(8,128)S(1)} %bitcast.15, s32[512,512]{1,0:T(8,128)S(1)} %copy-done.2, s32[512,512]{1,0:T(8,128)S(1)} %bitcast.13, bf16[256,256]{1,0:T(8,128)(2,1)S(1)} %copy-done.7), custom_call_target="tpu_custom_call" | custom-call | tf_op jit(solution)/shard_map/rotate/pallas_call | solution.py:91
  7.2 0.0 copy-start.8
  7.2 0.8 copy-done.8
  8.0 8.9 %collective-permute-start = (f32[520,512]{1,0:T(8,128)S(1)}, f32[520,512]{1,0:T(8,128)S(1)}, u32[]{:S(2)}, u32[]{:S(2)}) collective-permute-start(f32[520,512]{1,0:T(8,128)S(1)} %get-tuple-element.6.mine), channel_id=1, source_target_pairs={{0,8},{8,0},{1,9},{9,1},{2,10},{10,2},{3,11},{11,3},{4,12},{12,4},... | collective-permute-start | bytes 3194888 | tf_op jit(solution)/shard_map/ppermute | solution.py:211
  16.9 2.3 %collective-permute-done.theirs.other.other_dither = f32[520,512]{1,0:T(8,128)S(1)} collective-permute-done((f32[520,512]{1,0:T(8,128)S(1)}, f32[520,512]{1,0:T(8,128)S(1)}, u32[]{:S(2)}, u32[]{:S(2)}) %collective-permute-start) | collective-permute-done | bytes 1064992 | tf_op jit(solution)/shard_map/ppermute | solution.py:211
  19.2 1.0 copy-done
  20.2 1.5 %chip_top.1 = f32[256,128]{1,0:T(8,128)} custom-call(f32[520,512]{1,0:T(8,128)} %copy-done.5, f32[520,512]{1,0:T(8,128)} %copy-done), custom_call_target="tpu_custom_call" | custom-call | tf_op jit(solution)/shard_map/chip_top/pallas_call | solution.py:124
  21.7 28.8 %all_to_all.15 = f32[256,1,128]{2,1,0:T(1,128)S(1)} all-to-all(f32[256,1,128]{2,1,0:T(1,128)} %bitcast.19), channel_id=1, replica_groups=mesh['x'=4,'z'=8,'core'=2,'tensor'=8] {'x','z','tensor'}, dimensions={0} | all-to-all | bytes 262144 | tf_op jit(solution)/shard_map/all_to_all | solution.py:214
  50.5 0.0 copy-done.4
  50.5 1.2 %copy-done.1 = f32[520,512]{1,0:T(8,128)S(1)} copy-done((f32[520,512]{1,0:T(8,128)S(1)}, f32[520,512]{1,0:T(8,128)}, u32[]{:S(2)}) %copy-start.1) | copy-done | bytes 1064984
  51.7 1.0 copy-done.9
  52.7 1.4 %chip_codes.1 = (f32[256,512]{1,0:T(8,128)S(1)}, f32[1,1]{1,0:T(1,128)}) custom-call(s32[2]{0:T(128)S(1)} %pad_add_fusion.place.refs_0_, f32[256,128]{1,0:T(8,128)S(1)} %bitcast.16, f32[256,512]{1,0:T(8,128)S(1)} %copy-done.9, s32[512,512]{1,0:T(8,128)S(1)} %bitcast.14, f32[520,512]{1,0:T(8,128)S(1)} %copy-done.1, f32[520,512]{1,0:T(8,128)S(1)} %copy-done.1), custom_call_target="tpu_custom_call" | custom-call | tf_op jit(solution)/shard_map/chip_codes/pallas_call | solution.py:147
  54.2 16.8 %all_to_all.16.refs_1_ = f32[32,8,512]{2,1,0:T(8,128)} all-to-all(f32[32,8,512]{2,1,0:T(8,128)S(1)} %bitcast.17), channel_id=1, replica_groups=mesh['x'=4,'z'=8,'core'=2,'tensor'=8] {'x','z'}, dimensions={0} | all-to-all | bytes 1048576 | tf_op jit(solution)/shard_map/all_to_all | solution.py:218
  71.0 3.4 %owned_mean.1 = f32[32,8,512]{2,1,0:T(8,128)} custom-call(s32[2]{0:T(128)} %copy-done.10, f32[32,8,512]{2,1,0:T(8,128)} %all_to_all.16.refs_1_, s32[512,512]{1,0:T(8,128)} %refs_2_.1, bf16[256,256]{1,0:T(8,128)(2,1)} %constant.23.clone.matrix.refs_3_, f32[1,1]{1,0:T(1,128)} %get-tuple-element.9.refs_4_), custom_call_target="tpu_custom_call" | custom-call | tf_op jit(solution)/shard_map/owned_mean/pallas_call | solution.py:183
  74.4 20.2 %all_to_all.17 = f32[32,8,512]{2,1,0:T(8,128)S(1)} all-to-all(f32[32,8,512]{2,1,0:T(8,128)} %owned_mean.1), channel_id=1, replica_groups=mesh['x'=4,'z'=8,'core'=2,'tensor'=8] {'x','z'}, dimensions={0} | all-to-all | bytes 1048576 | tf_op jit(solution)/shard_map/all_to_all | solution.py:221
  94.6 7.2 %collective-permute-start.1 = (f32[256,512]{1,0:T(8,128)S(1)}, f32[256,512]{1,0:T(8,128)S(1)}, u32[]{:S(2)}, u32[]{:S(2)}) collective-permute-start(f32[256,512]{1,0:T(8,128)S(1)} %bitcast.18), channel_id=1, source_target_pairs={{0,8},{8,0},{1,9},{9,1},{2,10},{10,2},{3,11},{11,3},{4,12},{12,4},... | collective-permute-start | bytes 1572872 | tf_op jit(solution)/shard_map/ppermute | solution.py:223
  101.8 1.5 %collective-permute-done.1 = f32[256,512]{1,0:T(8,128)S(1)} collective-permute-done((f32[256,512]{1,0:T(8,128)S(1)}, f32[256,512]{1,0:T(8,128)S(1)}, u32[]{:S(2)}, u32[]{:S(2)}) %collective-permute-start.1) | collective-permute-done | bytes 524320 | tf_op jit(solution)/shard_map/ppermute | solution.py:223
  103.4 0.1 broadcast_select_fusion.1
  103.5 1.0 pad_maximum_fusion
  (12 shorter events, 0.0 us)
Async XLA Ops:
  0.7 49.7 %copy-start.10 = (s32[2]{0:T(128)}, s32[2]{0:T(128)S(1)}, u32[]{:S(2)}) copy-start(s32[2]{0:T(128)S(1)} %pad_add_fusion.place.refs_0_) | copy-start | bytes 28
  0.7 1.2 %copy-start.2 = (s32[512,512]{1,0:T(8,128)S(1)}, s32[512,512]{1,0:T(8,128)}, u32[]{:S(2)}) copy-start(s32[512,512]{1,0:T(8,128)} %refs_2_.1) | copy-start | bytes 3145732
  1.9 1.2 %copy-start.3 = (s32[1,512,512]{2,1,0:T(8,128)S(1)}, s32[1,512,512]{2,1,0:T(8,128)}, u32[]{:S(2)}) copy-start(s32[1,512,512]{2,1,0:T(8,128)} %param.6) | copy-start | bytes 3145732
  3.2 1.2 %copy-start.6 = (f32[1,512,512]{2,1,0:T(8,128)S(1)}, f32[1,512,512]{2,1,0:T(8,128)}, u32[]{:S(2)}) copy-start(f32[1,512,512]{2,1,0:T(8,128)} %param.4) | copy-start | bytes 3145732
  4.4 0.9 copy-start.7
  7.2 0.8 copy-start.8
  8.0 11.2 %copy-start.5 = (f32[520,512]{1,0:T(8,128)}, f32[520,512]{1,0:T(8,128)S(1)}, u32[]{:S(2)}) copy-start(f32[520,512]{1,0:T(8,128)S(1)} %get-tuple-element.6.mine) | copy-start | bytes 3194884
  8.0 42.5 %copy-start.4 = (s32[1,512,512]{2,1,0:T(8,128)S(1)}, s32[1,512,512]{2,1,0:T(8,128)}, u32[]{:S(2)}) copy-start(s32[1,512,512]{2,1,0:T(8,128)} %param.6) | copy-start | bytes 3145732
  8.0 11.2 %collective-permute-start = (f32[520,512]{1,0:T(8,128)S(1)}, f32[520,512]{1,0:T(8,128)S(1)}, u32[]{:S(2)}, u32[]{:S(2)}) collective-permute-start(f32[520,512]{1,0:T(8,128)S(1)} %get-tuple-element.6.mine), channel_id=1, source_target_pairs={{0,8},{8,0},{1,9},{9,1},{2,10},{10,2},{3,11},{11,3},{4,12},{12,4},... | collective-permute-start | bytes 3194888 | tf_op jit(solution)/shard_map/ppermute | solution.py:211
  19.2 1.0 copy-start
  50.5 1.2 %copy-start.1 = (f32[520,512]{1,0:T(8,128)S(1)}, f32[520,512]{1,0:T(8,128)}, u32[]{:S(2)}) copy-start(f32[520,512]{1,0:T(8,128)} %copy-done) | copy-start | bytes 3194884
  51.7 1.0 copy-start.9
  94.6 8.7 %collective-permute-start.1 = (f32[256,512]{1,0:T(8,128)S(1)}, f32[256,512]{1,0:T(8,128)S(1)}, u32[]{:S(2)}, u32[]{:S(2)}) collective-permute-start(f32[256,512]{1,0:T(8,128)S(1)} %bitcast.18), channel_id=1, source_target_pairs={{0,8},{8,0},{1,9},{9,1},{2,10},{10,2},{3,11},{11,3},{4,12},{12,4},... | collective-permute-start | bytes 1572872 | tf_op jit(solution)/shard_map/ppermute | solution.py:223

commit v2 on v1

v2 whole, which is shorter than its diff:
```python
import math

import jax
import jax.numpy as jnp
import numpy as np
from jax import lax
from jax.experimental import pallas as pl
from jax.experimental.pallas import tpu as pltpu
from jax.sharding import Mesh, PartitionSpec as P

Z, CORES = 8, 2
CHIPS = ("x", "z")
STRIPE = 128


def signs_matrix(length):
    matrix = np.ones((1, 1), np.float32)
    while matrix.shape[0] < length:
        matrix = np.block([[matrix, matrix], [matrix, -matrix]])
    return jnp.asarray(matrix, jnp.bfloat16)


def butterfly(values):
    half = values.shape[1] // 2
    left, right = values[:, :half], values[:, half:]
    return jnp.concatenate([left + right, left - right], axis=0)


def parts_of(values, count):
    parts = []
    for _ in range(count):
        part = values.astype(jnp.bfloat16)
        parts.append(part)
        values = values - part.astype(jnp.float32)
    return parts


def transform(values, matrix, count):
    rows, length = values.shape
    parts = parts_of(butterfly(values), count)
    out = jnp.dot(parts[-1], matrix, preferred_element_type=jnp.float32)
    for part in parts[-2::-1]:
        out = out + jnp.dot(part, matrix, preferred_element_type=jnp.float32)
    out = out * (1.0 / math.sqrt(length))
    return jnp.concatenate([out[:rows], out[rows:]], axis=1)


def rotate_kernel(
    place, grads, signs, dither, matrix_in, own, own_dither, send, matrix, own_signs,
    grads_buf, signs_buf, dither_buf, fetched, kept,
):
    rows, length = grads.shape
    half = rows // 2
    steps = half // STRIPE
    mine = place[0] * half
    others = half - mine
    starts = [others + i * STRIPE for i in range(steps)] + [mine + i * STRIPE for i in range(steps)]

    def fetch(i, which):
        at = pl.multiple_of(starts[i], STRIPE)
        source, target = ((grads, grads_buf), (signs, signs_buf), (dither, dither_buf))[which]
        return pltpu.make_async_copy(
            source.at[pl.ds(at, STRIPE), :], target.at[pl.ds(i * STRIPE, STRIPE), :], fetched.at[which, i]
        )

    copies = [[fetch(i, which) for which in range(3 if i < steps else 2)] for i in range(2 * steps)]
    get_matrix = pltpu.make_async_copy(matrix_in, matrix, kept.at[0])
    get_dither = pltpu.make_async_copy(
        dither.at[pl.ds(pl.multiple_of(mine, STRIPE), half), :], own_dither, kept.at[1]
    )
    for i, group in enumerate(copies):
        group[0].start()
        group[1].start()
        if i == 0:
            get_matrix.start()
    for group in copies[:steps]:
        group[2].start()
    get_dither.start()
    get_matrix.wait()

    top = None
    for i, group in enumerate(copies):
        here = pl.ds(i * STRIPE, STRIPE)
        group[0].wait()
        group[1].wait()
        rotated = transform(grads_buf[here, :] * signs_buf[here, :].astype(jnp.float32), matrix[...], 3)
        highest = jnp.max(jnp.abs(rotated).reshape(STRIPE // 8, 8, length), axis=0)
        top = highest if top is None else jnp.maximum(top, highest)
        if i < steps:
            send[here, :] = rotated
        else:
            own[pl.ds((i - steps) * STRIPE, STRIPE), :] = rotated
    send[rows:, :] = top
    for i, group in enumerate(copies[:steps]):
        group[2].wait()
        here = pl.ds(i * STRIPE, STRIPE)
        send[pl.ds(half + i * STRIPE, STRIPE), :] = dither_buf[here, :].astype(jnp.float32)
    mean_rows = own_signs.shape[0]
    at = pl.multiple_of(half + place[1] * mean_rows, mean_rows)
    own_signs[...] = signs_buf[pl.ds(at, mean_rows), :].astype(jnp.float32)
    get_dither.wait()


VMEM = pl.BlockSpec(memory_space=pltpu.VMEM)
SMEM = pl.BlockSpec(memory_space=pltpu.SMEM)
HBM = pl.BlockSpec(memory_space=pltpu.HBM)
LIMIT = pltpu.CompilerParams(vmem_limit_bytes=16 * 2**20)


def rotate(place, grads, signs, dither, matrix, mean_rows):
    rows, length = grads.shape
    half = rows // 2
    steps = half // STRIPE
    return pl.pallas_call(
        rotate_kernel,
        in_specs=[SMEM, HBM, HBM, HBM, HBM],
        out_specs=[VMEM] * 5,
        out_shape=[
            jax.ShapeDtypeStruct((half, length), jnp.float32),
            jax.ShapeDtypeStruct((half, length), jnp.int32),
            jax.ShapeDtypeStruct((rows + 8, length), jnp.float32),
            jax.ShapeDtypeStruct(matrix.shape, matrix.dtype),
            jax.ShapeDtypeStruct((mean_rows, length), jnp.float32),
        ],
        scratch_shapes=[
            pltpu.VMEM((rows, length), jnp.float32),
            pltpu.VMEM((rows, length), jnp.int32),
            pltpu.VMEM((half, length), jnp.int32),
            pltpu.SemaphoreType.DMA((3, 2 * steps)),
            pltpu.SemaphoreType.DMA((2,)),
        ],
        compiler_params=LIMIT,
        name="rotate",
    )(place, *(pltpu.with_memory_space_constraint(a, pltpu.HBM) for a in (grads, signs, dither, matrix)))


def chip_top_kernel(sent, received, out):
    last = pl.ds(sent.shape[0] - 8, 8)
    top = jnp.max(jnp.maximum(sent[last, :], received[last, :]))
    out[...] = jnp.full(out.shape, top, jnp.float32)


def chip_top(sent, received, peers):
    return pl.pallas_call(
        chip_top_kernel,
        in_specs=[VMEM, VMEM],
        out_specs=VMEM,
        out_shape=jax.ShapeDtypeStruct((peers, 128), jnp.float32),
        compiler_params=LIMIT,
        name="chip_top",
    )(sent, received)


def codes_kernel(tops, own, dither, received, codes, quant_step):
    half, length = own.shape
    top = jnp.max(tops[...], axis=0, keepdims=True)
    scale = jnp.concatenate([127.0 / top] * (length // 128), axis=1)
    for i in range(0, half, STRIPE):
        here, there = pl.ds(i, STRIPE), pl.ds(half + i, STRIPE)
        first = jnp.floor(own[here, :] * scale + dither[here, :].astype(jnp.float32) * 2.0 ** (-12))
        second = jnp.floor(received[here, :] * scale + received[there, :] * 2.0 ** (-12))
        codes[here, :] = first + second
    quant_step[0, 0] = jnp.max(top / 127.0)


def chip_codes(tops, own, dither, received):
    return pl.pallas_call(
        codes_kernel,
        in_specs=[VMEM] * 4,
        out_specs=[VMEM, SMEM],
        out_shape=[
            jax.ShapeDtypeStruct(own.shape, jnp.float32),
            jax.ShapeDtypeStruct((1, 1), jnp.float32),
        ],
        compiler_params=LIMIT,
        name="chip_codes",
    )(tops, own, dither, received)


def mean_kernel(replicas, codes, signs, matrix, quant_step, out):
    total = jnp.sum(codes[...], axis=0)
    back = transform(total, matrix[...], 2)
    mean = signs[...] * (back * (quant_step[0, 0] * (1.0 / replicas)))
    out[...] = jnp.broadcast_to(mean[None], out.shape)


def owned_mean(replicas, codes, signs, matrix, quant_step):
    return pl.pallas_call(
        lambda *refs: mean_kernel(replicas, *refs),
        in_specs=[VMEM, VMEM, VMEM, SMEM],
        out_specs=VMEM,
        out_shape=jax.ShapeDtypeStruct(codes.shape, jnp.float32),
        compiler_params=LIMIT,
        name="owned_mean",
    )(codes, signs, matrix, quant_step)


PIECES = 4


def store_half(place, half, out, done, which):
    rows = half.shape[0]
    core = place[0] if which == 0 else 1 - place[0]
    piece = rows // PIECES
    copies = [
        pltpu.make_async_copy(
            half.at[pl.ds(i * piece, piece), :],
            out.at[pl.ds(pl.multiple_of(core * rows + i * piece, piece), piece), :],
            done.at[i],
        )
        for i in range(PIECES)
    ]
    for copy in copies:
        copy.start()
    for copy in copies:
        copy.wait()


def store_mine_kernel(place, half, out, done):
    store_half(place, half, out, done, 0)


def store_other_kernel(place, half, _, out, done):
    store_half(place, half, out, done, 1)


def store_mine(place, half):
    rows, length = half.shape
    return pl.pallas_call(
        store_mine_kernel,
        in_specs=[SMEM, VMEM],
        out_specs=HBM,
        out_shape=jax.ShapeDtypeStruct((2 * rows, length), half.dtype),
        scratch_shapes=[pltpu.SemaphoreType.DMA((PIECES,))],
        compiler_params=LIMIT,
        name="store_mine",
    )(place, half)


def store_other(place, half, out):
    return pl.pallas_call(
        store_other_kernel,
        in_specs=[SMEM, VMEM, HBM],
        out_specs=HBM,
        out_shape=jax.ShapeDtypeStruct(out.shape, out.dtype),
        scratch_shapes=[pltpu.SemaphoreType.DMA((PIECES,))],
        input_output_aliases={2: 0},
        compiler_params=LIMIT,
        name="store_other",
    )(place, half, out)


def shards(grads, signs, dither):
    _, rows, length = grads.shape
    chips = lax.axis_size(CHIPS)
    peers = lax.axis_size(CHIPS + ("tensor",))
    core = lax.axis_index("core")
    place = jnp.stack([core, lax.axis_index(CHIPS)]).astype(jnp.int32)
    swap = [(0, 1), (1, 0)]
    matrix = signs_matrix(length // 2)
    mean_rows = rows // 2 // chips

    own, own_dither, send, matrix, own_signs = rotate(place, grads[0], signs, dither[0], matrix, mean_rows)
    received = lax.ppermute(send, "core", swap)

    tops = chip_top(send, received, peers).reshape(peers, 1, 128)
    tops = lax.all_to_all(tops, CHIPS + ("tensor",), 0, 0).reshape(peers, 128)

    codes, quant_step = chip_codes(tops, own, own_dither, received)
    codes = lax.all_to_all(codes.reshape(chips, mean_rows, length), CHIPS, 0, 0)

    mean = owned_mean(CORES * chips, codes, own_signs, matrix, quant_step)
    mean = lax.all_to_all(mean, CHIPS, 0, 0).reshape(rows // 2, length)

    other = lax.ppermute(mean, "core", swap)
    mean_grad = store_other(place, other, store_mine(place, mean))
    return (mean_grad, quant_step.reshape(()))


def solution(mesh):
    tensor = mesh.shape["tensor"]
    devices = mesh.devices.reshape(-1, Z, CORES, tensor)
    fine = Mesh(devices, ("x", "z", "core", "tensor"))
    dp = ("x", "z", "core")
    return jax.shard_map(
        shards,
        mesh=fine,
        in_specs=(P(dp, "tensor", None), P("tensor", None), P(dp, "tensor", None)),
        out_specs=(P("tensor", None), P()),
        check_vma=False,
    )
```

time: 105 us -> 93 us (0.89)
  local copies, waits for them, and re-layouts: 8.63 us -> 0 us
  waiting for transfers between devices: 3.8 us -> 2.43 us
  other arithmetic: 1.23 us -> 0.08 us
    unnamed x22 -> x0, local copies, waits for them, and re-layouts: 8.63 us -> none
    ppermute x1, waiting for transfers between devices: 1.51 us -> 0.14 us  [shards(): other = lax.ppermute(mean, 'core', swap)]
    pallas_call x4 -> x6, Pallas kernels: 8.19 us -> 8.11 us  [the longest x1 3.69 us: rotate(): pl.pallas_call(rotate_kernel, in_specs=[SMEM, HBM, HBM, HBM, HBM], out_sp...]
  transfers between devices with their start and end apart: 2 -> 2, of which waited for: 2 -> 2; matrix products, arithmetic and copies ran while one was open for 0% -> 0% of each run, Pallas kernels for 0% -> 1%
where the time goes in v2:
time: 93 us; the launch traced here: 92.7 us
  blocking collectives  65.4 us (70%)
  starting transfers between devices  16 us (17%)
  Pallas kernels  8.11 us (9%)
  waiting for transfers between devices  2.43 us (3%)
    all_to_all x1, blocking collectives, shards(): tops = lax.all_to_all(tops, CHIPS + ('tensor',), 0, 0).reshape(peers, 128)  28.6 us
    all_to_all x1, blocking collectives, shards(): mean = lax.all_to_all(mean, CHIPS, 0, 0).reshape(rows // 2, length)  20.1 us
    all_to_all x1, blocking collectives, shards(): codes = lax.all_to_all(codes.reshape(chips, mean_rows, length), CHIPS, 0, 0)  16.7 us
    ppermute x1, starting transfers between devices, shards(): received = lax.ppermute(send, 'core', swap)  8.79 us
    ppermute x1, starting transfers between devices, shards(): other = lax.ppermute(mean, 'core', swap)  7.19 us
    pallas_call x1, Pallas kernels, rotate(): pl.pallas_call(rotate_kernel, in_specs=[SMEM, HBM, HBM, HBM, HBM], out_sp...  3.69 us
    ppermute x1, waiting for transfers between devices, shards(): received = lax.ppermute(send, 'core', swap)  2.29 us
  transfers between devices with their start and end apart: 2, of which 2 were waited for; matrix products, arithmetic and copies ran while one was open for 0% of the time, Pallas kernels for 1%

profile of v2, /device:TPU:1, one launch (start us, length us, event | category | flops | bytes accessed | tf_op | source)
XLA Modules:
  0.0 92.7 jit_solution(7544260530539108513)
XLA Ops:
  0.6 0.1 pad_add_fusion.place
  0.7 3.7 %rotate.1 = (f32[256,512]{1,0:T(8,128)S(1)}, s32[256,512]{1,0:T(8,128)S(1)}, f32[520,512]{1,0:T(8,128)S(1)}, bf16[256,256]{1,0:T(8,128)(2,1)S(1)}, f32[8,512]{1,0:T(8,128)S(1)}) custom-call(s32[2]{0:T(128)S(1)} %pad_add_fusion.place, f32[512,512]{1,0:T(8,128)} %bitcast.16, s32[512,512]{1,0:T(8,128)} %signs.1, s32[512,512]{1,0:T(8,128)} %bitcast.17, ...), custom_call_target="tpu_custom_call" | custom-call | tf_op jit(solution)/shard_map/rotate/pallas_call | solution.py:114
  4.4 8.8 %collective-permute-start = (f32[520,512]{1,0:T(8,128)S(1)}, f32[520,512]{1,0:T(8,128)S(1)}, u32[]{:S(2)}, u32[]{:S(2)}) collective-permute-start(f32[520,512]{1,0:T(8,128)S(1)} %get-tuple-element.9.sent), channel_id=1, source_target_pairs={{0,8},{8,0},{1,9},{9,1},{2,10},{10,2},{3,11},{11,3},{4,12},{12,4},... | collective-permute-start | bytes 3194888 | tf_op jit(solution)/shard_map/ppermute | solution.py:264
  13.2 2.3 %collective-permute-done.received = f32[520,512]{1,0:T(8,128)S(1)} collective-permute-done((f32[520,512]{1,0:T(8,128)S(1)}, f32[520,512]{1,0:T(8,128)S(1)}, u32[]{:S(2)}, u32[]{:S(2)}) %collective-permute-start) | collective-permute-done | bytes 1064992 | tf_op jit(solution)/shard_map/ppermute | solution.py:264
  15.5 0.1 chip_top.1
  15.6 28.6 %all_to_all.15 = f32[256,1,128]{2,1,0:T(1,128)S(1)} all-to-all(f32[256,1,128]{2,1,0:T(1,128)S(1)} %bitcast.14), channel_id=1, replica_groups=mesh['x'=4,'z'=8,'core'=2,'tensor'=8] {'x','z','tensor'}, dimensions={0} | all-to-all | bytes 262144 | tf_op jit(solution)/shard_map/all_to_all | solution.py:267
  44.2 0.7 chip_codes.1
  44.9 16.7 %all_to_all.16.refs_0_ = f32[32,8,512]{2,1,0:T(8,128)S(1)} all-to-all(f32[32,8,512]{2,1,0:T(8,128)S(1)} %bitcast.15), channel_id=1, replica_groups=mesh['x'=4,'z'=8,'core'=2,'tensor'=8] {'x','z'}, dimensions={0} | all-to-all | bytes 1048576 | tf_op jit(solution)/shard_map/all_to_all | solution.py:270
  61.7 0.9 owned_mean.1
  62.6 20.1 %all_to_all.17 = f32[32,8,512]{2,1,0:T(8,128)S(1)} all-to-all(f32[32,8,512]{2,1,0:T(8,128)S(1)} %owned_mean.1), channel_id=1, replica_groups=mesh['x'=4,'z'=8,'core'=2,'tensor'=8] {'x','z'}, dimensions={0} | all-to-all | bytes 1048576 | tf_op jit(solution)/shard_map/all_to_all | solution.py:273
  82.6 7.2 %collective-permute-start.1 = (f32[256,512]{1,0:T(8,128)S(1)}, f32[256,512]{1,0:T(8,128)S(1)}, u32[]{:S(2)}, u32[]{:S(2)}) collective-permute-start(f32[256,512]{1,0:T(8,128)S(1)} %bitcast.11), channel_id=1, source_target_pairs={{0,8},{8,0},{1,9},{9,1},{2,10},{10,2},{3,11},{11,3},{4,12},{12,4},... | collective-permute-start | bytes 1572872 | tf_op jit(solution)/shard_map/ppermute | solution.py:275
  89.8 1.4 %store_mine.1._ = f32[512,512]{1,0:T(8,128)} custom-call(s32[2]{0:T(128)S(1)} %pad_add_fusion.place, f32[256,512]{1,0:T(8,128)S(1)} %bitcast.12), custom_call_target="tpu_custom_call" | custom-call | tf_op jit(solution)/shard_map/store_mine/pallas_call | solution.py:229
  91.2 0.1 collective-permute-done.1.half
  91.3 1.4 %store_other.1 = f32[512,512]{1,0:T(8,128)} custom-call(s32[2]{0:T(128)S(1)} %pad_add_fusion.place, f32[256,512]{1,0:T(8,128)S(1)} %collective-permute-done.1.half, f32[512,512]{1,0:T(8,128)} %store_mine.1._), custom_call_target="tpu_custom_call", output_to_operand_aliasing={{}: (2, {})} | custom-call | tf_op jit(solution)/shard_map/store_other/pallas_call | solution.py:241
Async XLA Ops:
  4.4 11.1 %collective-permute-start = (f32[520,512]{1,0:T(8,128)S(1)}, f32[520,512]{1,0:T(8,128)S(1)}, u32[]{:S(2)}, u32[]{:S(2)}) collective-permute-start(f32[520,512]{1,0:T(8,128)S(1)} %get-tuple-element.9.sent), channel_id=1, source_target_pairs={{0,8},{8,0},{1,9},{9,1},{2,10},{10,2},{3,11},{11,3},{4,12},{12,4},... | collective-permute-start | bytes 3194888 | tf_op jit(solution)/shard_map/ppermute | solution.py:264
  82.6 8.7 %collective-permute-start.1 = (f32[256,512]{1,0:T(8,128)S(1)}, f32[256,512]{1,0:T(8,128)S(1)}, u32[]{:S(2)}, u32[]{:S(2)}) collective-permute-start(f32[256,512]{1,0:T(8,128)S(1)} %bitcast.11), channel_id=1, source_target_pairs={{0,8},{8,0},{1,9},{9,1},{2,10},{10,2},{3,11},{11,3},{4,12},{12,4},... | collective-permute-start | bytes 1572872 | tf_op jit(solution)/shard_map/ppermute | solution.py:275

commit v3 on v2

v3 whole, which is shorter than its diff:
```python
import math

import jax
import jax.numpy as jnp
import numpy as np
from jax import lax
from jax.experimental import pallas as pl
from jax.experimental.pallas import tpu as pltpu
from jax.sharding import Mesh, PartitionSpec as P

Z, CORES = 8, 2
CHIPS = ("x", "z")
NEAR, FAR = ("core", "tensor"), ("x", "z")
STRIPE = 64


def signs_matrix(length):
    matrix = np.ones((1, 1), np.float32)
    while matrix.shape[0] < length:
        matrix = np.block([[matrix, matrix], [matrix, -matrix]])
    return jnp.asarray(matrix, jnp.bfloat16)


def butterfly(values):
    half = values.shape[1] // 2
    left, right = values[:, :half], values[:, half:]
    return jnp.concatenate([left + right, left - right], axis=0)


def parts_of(values, count):
    parts = []
    for _ in range(count):
        part = values.astype(jnp.bfloat16)
        parts.append(part)
        values = values - part.astype(jnp.float32)
    return parts


def transform(values, matrix, count):
    rows, length = values.shape
    parts = jnp.concatenate(parts_of(butterfly(values), count), axis=0)
    products = jnp.dot(parts, matrix, preferred_element_type=jnp.float32)
    out = products[-2 * rows :]
    for i in range(count - 2, -1, -1):
        out = out + products[2 * rows * i : 2 * rows * (i + 1)]
    out = out * (1.0 / math.sqrt(length))
    return jnp.concatenate([out[:rows], out[rows:]], axis=1)


def rotate_kernel(
    grads, signs, dither, matrix_in, own, own_dither, send, tops, matrix, own_signs,
    grads_buf, signs_buf, dither_buf, fetched, kept,
):
    rows, length = grads.shape
    half = rows // 2
    mine = lax.axis_index("core") * half
    others = half - mine
    low, high = pl.ds(0, half), pl.ds(half, half)

    def at(start):
        return pl.ds(pl.multiple_of(start, half), half)

    def fetch(source, start, target, place, semaphore):
        return pltpu.make_async_copy(source.at[at(start), :], target.at[place, :], semaphore)

    stages = [
        (place, fetch(grads, start, grads_buf, place, fetched.at[0, i]), fetch(signs, start, signs_buf, place, fetched.at[1, i]))
        for i, (place, start) in enumerate(((low, others), (high, mine)))
    ]
    get_matrix = pltpu.make_async_copy(matrix_in, matrix, kept.at[0])
    get_others = pltpu.make_async_copy(dither.at[at(others), :], dither_buf, kept.at[1])
    get_mine = pltpu.make_async_copy(dither.at[at(mine), :], own_dither, kept.at[2])
    get_matrix.start()
    for _, get_grads, get_signs in stages:
        get_grads.start()
        get_signs.start()
    get_others.start()
    get_mine.start()
    get_matrix.wait()

    top = jnp.zeros((8, length), jnp.float32)
    for (place, get_grads, get_signs), result in zip(stages, (send, own)):
        get_grads.wait()
        get_signs.wait()
        rotated = transform(grads_buf[place, :] * signs_buf[place, :].astype(jnp.float32), matrix[...], 3)
        top = jnp.maximum(top, jnp.max(jnp.abs(rotated).reshape(half // 8, 8, length), axis=0))
        result[low, :] = rotated
    tops[...] = jnp.full(tops.shape, jnp.max(top), jnp.float32)
    get_others.wait()
    send[high, :] = dither_buf[...].astype(jnp.float32)
    mean_rows = own_signs.shape[0]
    chip = lax.axis_index("x") * lax.axis_size("z") + lax.axis_index("z")
    here = pl.ds(pl.multiple_of(half + chip * mean_rows, mean_rows), mean_rows)
    own_signs[...] = signs_buf[here, :].astype(jnp.float32)
    get_mine.wait()


VMEM = pl.BlockSpec(memory_space=pltpu.VMEM)
SMEM = pl.BlockSpec(memory_space=pltpu.SMEM)
HBM = pl.BlockSpec(memory_space=pltpu.HBM)
LIMIT = pltpu.CompilerParams(vmem_limit_bytes=16 * 2**20)


def rotate(grads, signs, dither, matrix, mean_rows, peers):
    rows, length = grads.shape
    half = rows // 2
    return pl.pallas_call(
        rotate_kernel,
        in_specs=[HBM] * 4,
        out_specs=[VMEM] * 6,
        out_shape=[
            jax.ShapeDtypeStruct((half, length), jnp.float32),
            jax.ShapeDtypeStruct((half, length), jnp.int32),
            jax.ShapeDtypeStruct((rows, length), jnp.float32),
            jax.ShapeDtypeStruct((peers, 128), jnp.float32),
            jax.ShapeDtypeStruct(matrix.shape, matrix.dtype),
            jax.ShapeDtypeStruct((mean_rows, length), jnp.float32),
        ],
        scratch_shapes=[
            pltpu.VMEM((rows, length), jnp.float32),
            pltpu.VMEM((rows, length), jnp.int32),
            pltpu.VMEM((half, length), jnp.int32),
            pltpu.SemaphoreType.DMA((2, 2)),
            pltpu.SemaphoreType.DMA((3,)),
        ],
        compiler_params=LIMIT,
        name="rotate",
    )(*(pltpu.with_memory_space_constraint(a, pltpu.HBM) for a in (grads, signs, dither, matrix)))


def highest_kernel(tops, out):
    out[...] = jnp.broadcast_to(jnp.max(tops[...], axis=0, keepdims=True), out.shape)


def highest(tops, peers):
    return pl.pallas_call(
        highest_kernel,
        in_specs=[VMEM],
        out_specs=VMEM,
        out_shape=jax.ShapeDtypeStruct((peers, 128), jnp.float32),
        compiler_params=LIMIT,
        name="highest",
    )(tops)


def exchange(tops, axes):
    peers, lanes = tops.shape
    return lax.all_to_all(tops.reshape(peers, 1, lanes), axes, 0, 0).reshape(peers, lanes)


def codes_kernel(tops, own, dither, received, codes, quant_step):
    half, length = own.shape
    top = jnp.max(tops[...], axis=0, keepdims=True)
    scale = jnp.concatenate([127.0 / top] * (length // 128), axis=1)
    for i in range(0, half, STRIPE):
        here, there = pl.ds(i, STRIPE), pl.ds(half + i, STRIPE)
        first = jnp.floor(own[here, :] * scale + dither[here, :].astype(jnp.float32) * 2.0 ** (-12))
        second = jnp.floor(received[here, :] * scale + received[there, :] * 2.0 ** (-12))
        codes[here, :] = first + second
    quant_step[0, 0] = jnp.max(top / 127.0)


def chip_codes(tops, own, dither, received):
    return pl.pallas_call(
        codes_kernel,
        in_specs=[VMEM] * 4,
        out_specs=[VMEM, SMEM],
        out_shape=[
            jax.ShapeDtypeStruct(own.shape, jnp.float32),
            jax.ShapeDtypeStruct((1, 1), jnp.float32),
        ],
        compiler_params=LIMIT,
        name="chip_codes",
    )(tops, own, dither, received)


def mean_kernel(replicas, codes, signs, matrix, quant_step, out):
    total = jnp.sum(codes[...], axis=0)
    back = transform(total, matrix[...], 2)
    mean = signs[...] * (back * (quant_step[0, 0] * (1.0 / replicas)))
    out[...] = jnp.broadcast_to(mean[None], out.shape)


def owned_mean(replicas, codes, signs, matrix, quant_step):
    return pl.pallas_call(
        lambda *refs: mean_kernel(replicas, *refs),
        in_specs=[VMEM, VMEM, VMEM, SMEM],
        out_specs=VMEM,
        out_shape=jax.ShapeDtypeStruct(codes.shape, jnp.float32),
        compiler_params=LIMIT,
        name="owned_mean",
    )(codes, signs, matrix, quant_step)


def store(half, out, done, core):
    rows = half.shape[0]
    copy = pltpu.make_async_copy(half, out.at[pl.ds(pl.multiple_of(core * rows, rows), rows), :], done)
    copy.start()
    copy.wait()


def store_mine_kernel(half, out, done):
    store(half, out, done, lax.axis_index("core"))


def store_other_kernel(half, _, out, done):
    store(half, out, done, 1 - lax.axis_index("core"))


def store_mine(half):
    rows, length = half.shape
    return pl.pallas_call(
        store_mine_kernel,
        in_specs=[VMEM],
        out_specs=HBM,
        out_shape=jax.ShapeDtypeStruct((2 * rows, length), half.dtype),
        scratch_shapes=[pltpu.SemaphoreType.DMA],
        compiler_params=LIMIT,
        name="store_mine",
    )(half)


def store_other(half, out):
    return pl.pallas_call(
        store_other_kernel,
        in_specs=[VMEM, HBM],
        out_specs=HBM,
        out_shape=jax.ShapeDtypeStruct(out.shape, out.dtype),
        scratch_shapes=[pltpu.SemaphoreType.DMA],
        input_output_aliases={1: 0},
        compiler_params=LIMIT,
        name="store_other",
    )(half, out)


def shards(grads, signs, dither):
    _, rows, length = grads.shape
    chips = lax.axis_size(CHIPS)
    swap = [(0, 1), (1, 0)]
    matrix = signs_matrix(length // 2)
    mean_rows = rows // 2 // chips

    own, own_dither, send, tops, matrix, own_signs = rotate(
        grads[0], signs, dither[0], matrix, mean_rows, lax.axis_size(NEAR)
    )
    received = lax.ppermute(send, "core", swap)

    tops = highest(exchange(tops, NEAR), lax.axis_size(FAR))
    tops = exchange(tops, FAR)

    codes, quant_step = chip_codes(tops, own, own_dither, received)
    codes = lax.all_to_all(codes.reshape(chips, mean_rows, length), CHIPS, 0, 0)

    mean = owned_mean(CORES * chips, codes, own_signs, matrix, quant_step)
    mean = lax.all_to_all(mean, CHIPS, 0, 0).reshape(rows // 2, length)

    other = lax.ppermute(mean, "core", swap)
    mean_grad = store_other(other, store_mine(mean))
    return (mean_grad, quant_step.reshape(()))


def solution(mesh):
    tensor = mesh.shape["tensor"]
    devices = mesh.devices.reshape(-1, Z, CORES, tensor)
    fine = Mesh(devices, ("x", "z", "core", "tensor"))
    dp = ("x", "z", "core")
    return jax.shard_map(
        shards,
        mesh=fine,
        in_specs=(P(dp, "tensor", None), P("tensor", None), P(dp, "tensor", None)),
        out_specs=(P("tensor", None), P()),
        check_vma=False,
    )
```

time: 93 us -> 89.1 us (0.958)
  Pallas kernels: 8.11 us -> 5.78 us
  waiting for transfers between devices: 2.43 us -> 0.7 us
    pallas_call x4, Pallas kernels: 6.55 us -> 4.24 us  [the longest x1 2.62 us: rotate(): pl.pallas_call(rotate_kernel, in_specs=[HBM] * 4, out_specs=[VMEM] * 6, o...]
    ppermute x1, waiting for transfers between devices: 2.29 us -> 0.01 us  [shards(): received = lax.ppermute(send, 'core', swap)]
    all_to_all x1 -> x2, blocking collectives: 28.6 us -> 29.9 us  [exchange(): lax.all_to_all(tops.reshape(peers, 1, lanes), axes, 0, 0)]
  transfers between devices with their start and end apart: 2 -> 2, of which waited for: 2 -> 1; matrix products, arithmetic and copies ran while one was open for 0% -> 0% of each run, Pallas kernels for 1% -> 1%
where the time goes in v3:
time: 89.1 us; the launch traced here: 88.7 us
  blocking collectives  65.6 us (74%)
  starting transfers between devices  16 us (18%)
  Pallas kernels  5.78 us (6%)
    all_to_all x2, blocking collectives, exchange(): lax.all_to_all(tops.reshape(peers, 1, lanes), axes, 0, 0)  29.9 us
    all_to_all x1, blocking collectives, shards(): mean = lax.all_to_all(mean, CHIPS, 0, 0).reshape(rows // 2, length)  19.7 us
    all_to_all x1, blocking collectives, shards(): codes = lax.all_to_all(codes.reshape(chips, mean_rows, length), CHIPS, 0, 0)  15.9 us
    ppermute x1, starting transfers between devices, shards(): received = lax.ppermute(send, 'core', swap)  8.79 us
    ppermute x1, starting transfers between devices, shards(): other = lax.ppermute(mean, 'core', swap)  7.24 us
    pallas_call x1, Pallas kernels, rotate(): pl.pallas_call(rotate_kernel, in_specs=[HBM] * 4, out_specs=[VMEM] * 6, o...  2.62 us
  transfers between devices with their start and end apart: 2, of which 1 were waited for; matrix products, arithmetic and copies ran while one was open for 0% of the time, Pallas kernels for 1%

profile of v3, /device:TPU:1, one launch (start us, length us, event | category | flops | bytes accessed | tf_op | source)
XLA Modules:
  0.0 88.7 jit_solution(11392948907021254317)
XLA Ops:
  0.6 2.6 %rotate.1 = (f32[256,512]{1,0:T(8,128)S(1)}, s32[256,512]{1,0:T(8,128)S(1)}, f32[512,512]{1,0:T(8,128)S(1)}, f32[16,128]{1,0:T(8,128)S(1)}, bf16[256,256]{1,0:T(8,128)(2,1)S(1)}, /*index=5*/f32[8,512]{1,0:T(8,128)S(1)}) custom-call(f32[512,512]{1,0:T(8,128)} %bitcast.20, s32[512,512]{1,0:T(8,128)} %signs.1, s32[512,512]{1,0:T(8,128)} %bitcast.21, ...), custom_call_target="tpu_custom_call" | custom-call | tf_op jit(solution)/shard_map/rotate/pallas_call | solution.py:107
  3.3 8.8 %collective-permute-start = (f32[512,512]{1,0:T(8,128)S(1)}, f32[512,512]{1,0:T(8,128)S(1)}, u32[]{:S(2)}, u32[]{:S(2)}) collective-permute-start(f32[512,512]{1,0:T(8,128)S(1)} %get-tuple-element.13), channel_id=1, source_target_pairs={{0,8},{8,0},{1,9},{9,1},{2,10},{10,2},{3,11},{11,3},{4,12},{12,4},... | collective-permute-start | bytes 3145736 | tf_op jit(solution)/shard_map/ppermute | solution.py:246
  12.1 9.4 %all_to_all.20 = f32[16,1,128]{2,1,0:T(1,128)S(1)} all-to-all(f32[16,1,128]{2,1,0:T(1,128)S(1)} %bitcast.19), channel_id=1, replica_groups=mesh['x'=4,'z'=8,'core'=2,'tensor'=8] {'core','tensor'}, dimensions={0} | all-to-all | bytes 16384 | tf_op jit(solution)/shard_map/all_to_all | solution.py:148
  21.4 20.5 %all_to_all.21 = f32[32,1,128]{2,1,0:T(1,128)S(1)} all-to-all(f32[32,1,128]{2,1,0:T(1,128)S(1)} %bitcast.17), channel_id=1, replica_groups=mesh['x'=4,'z'=8,'core'=2,'tensor'=8] {'x','z'}, dimensions={0} | all-to-all | bytes 32768 | tf_op jit(solution)/shard_map/all_to_all | solution.py:148
  42.0 0.0 collective-permute-done.received
  42.0 0.7 chip_codes.1
  42.7 15.9 %all_to_all.22.refs_0_ = f32[32,8,512]{2,1,0:T(8,128)S(1)} all-to-all(f32[32,8,512]{2,1,0:T(8,128)S(1)} %bitcast.15), channel_id=1, replica_groups=mesh['x'=4,'z'=8,'core'=2,'tensor'=8] {'x','z'}, dimensions={0} | all-to-all | bytes 1048576 | tf_op jit(solution)/shard_map/all_to_all | solution.py:252
  58.6 0.9 owned_mean.1
  59.5 19.7 %all_to_all.23 = f32[32,8,512]{2,1,0:T(8,128)S(1)} all-to-all(f32[32,8,512]{2,1,0:T(8,128)S(1)} %owned_mean.1), channel_id=1, replica_groups=mesh['x'=4,'z'=8,'core'=2,'tensor'=8] {'x','z'}, dimensions={0} | all-to-all | bytes 1048576 | tf_op jit(solution)/shard_map/all_to_all | solution.py:255
  79.2 7.2 %collective-permute-start.1 = (f32[256,512]{1,0:T(8,128)S(1)}, f32[256,512]{1,0:T(8,128)S(1)}, u32[]{:S(2)}, u32[]{:S(2)}) collective-permute-start(f32[256,512]{1,0:T(8,128)S(1)} %bitcast.13), channel_id=1, source_target_pairs={{0,8},{8,0},{1,9},{9,1},{2,10},{10,2},{3,11},{11,3},{4,12},{12,4},... | collective-permute-start | bytes 1572872 | tf_op jit(solution)/shard_map/ppermute | solution.py:257
  86.4 0.8 store_mine.1._
  87.2 0.7 collective-permute-done.1.half
  87.9 0.8 store_other.1
  (1 shorter events, 0.0 us)
Async XLA Ops:
  3.3 38.7 %collective-permute-start = (f32[512,512]{1,0:T(8,128)S(1)}, f32[512,512]{1,0:T(8,128)S(1)}, u32[]{:S(2)}, u32[]{:S(2)}) collective-permute-start(f32[512,512]{1,0:T(8,128)S(1)} %get-tuple-element.13), channel_id=1, source_target_pairs={{0,8},{8,0},{1,9},{9,1},{2,10},{10,2},{3,11},{11,3},{4,12},{12,4},... | collective-permute-start | bytes 3145736 | tf_op jit(solution)/shard_map/ppermute | solution.py:246
  79.2 8.8 %collective-permute-start.1 = (f32[256,512]{1,0:T(8,128)S(1)}, f32[256,512]{1,0:T(8,128)S(1)}, u32[]{:S(2)}, u32[]{:S(2)}) collective-permute-start(f32[256,512]{1,0:T(8,128)S(1)} %bitcast.13), channel_id=1, source_target_pairs={{0,8},{8,0},{1,9},{9,1},{2,10},{10,2},{3,11},{11,3},{4,12},{12,4},... | collective-permute-start | bytes 1572872 | tf_op jit(solution)/shard_map/ppermute | solution.py:257

commit v4 on v3

--- a/solution.py
+++ b/solution.py
@@ -148,7 +148,7 @@
     return lax.all_to_all(tops.reshape(peers, 1, lanes), axes, 0, 0).reshape(peers, lanes)
 
 
-def codes_kernel(tops, own, dither, received, codes, quant_step):
+def codes_kernel(tops, own, dither, received, codes):
     half, length = own.shape
     top = jnp.max(tops[...], axis=0, keepdims=True)
     scale = jnp.concatenate([127.0 / top] * (length // 128), axis=1)
@@ -157,39 +157,37 @@
         first = jnp.floor(own[here, :] * scale + dither[here, :].astype(jnp.float32) * 2.0 ** (-12))
         second = jnp.floor(received[here, :] * scale + received[there, :] * 2.0 ** (-12))
         codes[here, :] = first + second
-    quant_step[0, 0] = jnp.max(top / 127.0)
 
 
 def chip_codes(tops, own, dither, received):
     return pl.pallas_call(
         codes_kernel,
         in_specs=[VMEM] * 4,
-        out_specs=[VMEM, SMEM],
-        out_shape=[
-            jax.ShapeDtypeStruct(own.shape, jnp.float32),
-            jax.ShapeDtypeStruct((1, 1), jnp.float32),
-        ],
+        out_specs=VMEM,
+        out_shape=jax.ShapeDtypeStruct(own.shape, jnp.float32),
         compiler_params=LIMIT,
         name="chip_codes",
     )(tops, own, dither, received)
 
 
-def mean_kernel(replicas, codes, signs, matrix, quant_step, out):
+def mean_kernel(replicas, tops, codes, signs, matrix, out):
     total = jnp.sum(codes[...], axis=0)
     back = transform(total, matrix[...], 2)
-    mean = signs[...] * (back * (quant_step[0, 0] * (1.0 / replicas)))
+    factor = jnp.max(tops[...], axis=0, keepdims=True) / 127.0 * (1.0 / replicas)
+    factor = jnp.concatenate([factor] * (total.shape[1] // 128), axis=1)
+    mean = signs[...] * (back * factor)
     out[...] = jnp.broadcast_to(mean[None], out.shape)
 
 
-def owned_mean(replicas, codes, signs, matrix, quant_step):
+def owned_mean(replicas, tops, codes, signs, matrix):
     return pl.pallas_call(
         lambda *refs: mean_kernel(replicas, *refs),
-        in_specs=[VMEM, VMEM, VMEM, SMEM],
+        in_specs=[VMEM] * 4,
         out_specs=VMEM,
         out_shape=jax.ShapeDtypeStruct(codes.shape, jnp.float32),
         compiler_params=LIMIT,
         name="owned_mean",
-    )(codes, signs, matrix, quant_step)
+    )(tops, codes, signs, matrix)
 
 
 def store(half, out, done, core):
@@ -199,7 +197,8 @@
     copy.wait()
 
 
-def store_mine_kernel(half, out, done):
+def store_mine_kernel(half, tops, out, quant_step, done):
+    quant_step[0, 0] = jnp.max(tops[...] / 127.0)
     store(half, out, done, lax.axis_index("core"))
 
 
@@ -207,17 +206,20 @@
     store(half, out, done, 1 - lax.axis_index("core"))
 
 
-def store_mine(half):
+def store_mine(half, tops):
     rows, length = half.shape
     return pl.pallas_call(
         store_mine_kernel,
-        in_specs=[VMEM],
-        out_specs=HBM,
-        out_shape=jax.ShapeDtypeStruct((2 * rows, length), half.dtype),
+        in_specs=[VMEM, VMEM],
+        out_specs=[HBM, SMEM],
+        out_shape=[
+            jax.ShapeDtypeStruct((2 * rows, length), half.dtype),
+            jax.ShapeDtypeStruct((1, 1), jnp.float32),
+        ],
         scratch_shapes=[pltpu.SemaphoreType.DMA],
         compiler_params=LIMIT,
         name="store_mine",
-    )(half)
+    )(half, tops)
 
 
 def store_other(half, out):
@@ -248,14 +250,15 @@
     tops = highest(exchange(tops, NEAR), lax.axis_size(FAR))
     tops = exchange(tops, FAR)
 
-    codes, quant_step = chip_codes(tops, own, own_dither, received)
+    codes = chip_codes(tops, own, own_dither, received)
     codes = lax.all_to_all(codes.reshape(chips, mean_rows, length), CHIPS, 0, 0)
 
-    mean = owned_mean(CORES * chips, codes, own_signs, matrix, quant_step)
+    mean = owned_mean(CORES * chips, tops, codes, own_signs, matrix)
     mean = lax.all_to_all(mean, CHIPS, 0, 0).reshape(rows // 2, length)
 
     other = lax.ppermute(mean, "core", swap)
-    mean_grad = store_other(other, store_mine(mean))
+    mean_grad, quant_step = store_mine(mean, tops)
+    mean_grad = store_other(other, mean_grad)
     return (mean_grad, quant_step.reshape(()))
 
 

time: 89.1 us -> 87.9 us (0.987)
  transfers between devices with their start and end apart: 2 -> 2, of which waited for: 1 -> 1; matrix products, arithmetic and copies ran while one was open for 0% -> 0% of each run, Pallas kernels for 1% -> 2%
where the time goes in v4:
time: 87.9 us; the launch traced here: 87.6 us
  blocking collectives  65.6 us (75%)
  starting transfers between devices  16 us (18%)
  Pallas kernels  5.16 us (6%)
    all_to_all x2, blocking collectives, exchange(): lax.all_to_all(tops.reshape(peers, 1, lanes), axes, 0, 0)  29.9 us
    all_to_all x1, blocking collectives, shards(): mean = lax.all_to_all(mean, CHIPS, 0, 0).reshape(rows // 2, length)  19.7 us
    all_to_all x1, blocking collectives, shards(): codes = lax.all_to_all(codes.reshape(chips, mean_rows, length), CHIPS, 0, 0)  15.9 us
    ppermute x1, starting transfers between devices, shards(): received = lax.ppermute(send, 'core', swap)  8.79 us
    ppermute x1, starting transfers between devices, shards(): other = lax.ppermute(mean, 'core', swap)  7.24 us
    pallas_call x1, Pallas kernels, rotate(): pl.pallas_call(rotate_kernel, in_specs=[HBM] * 4, out_specs=[VMEM] * 6, o...  2.62 us
  transfers between devices with their start and end apart: 2, of which 1 were waited for; matrix products, arithmetic and copies ran while one was open for 0% of the time, Pallas kernels for 2%

profile of v4, /device:TPU:1, one launch (start us, length us, event | category | flops | bytes accessed | tf_op | source)
XLA Modules:
  0.0 87.6 jit_solution(35468480545555260)
XLA Ops:
  0.6 2.6 %rotate.1 = (f32[256,512]{1,0:T(8,128)S(1)}, s32[256,512]{1,0:T(8,128)S(1)}, f32[512,512]{1,0:T(8,128)S(1)}, f32[16,128]{1,0:T(8,128)S(1)}, bf16[256,256]{1,0:T(8,128)(2,1)S(1)}, /*index=5*/f32[8,512]{1,0:T(8,128)S(1)}) custom-call(f32[512,512]{1,0:T(8,128)} %bitcast.22, s32[512,512]{1,0:T(8,128)} %signs.1, s32[512,512]{1,0:T(8,128)} %bitcast.23, ...), custom_call_target="tpu_custom_call" | custom-call | tf_op jit(solution)/shard_map/rotate/pallas_call | solution.py:107
  3.3 8.8 %collective-permute-start = (f32[512,512]{1,0:T(8,128)S(1)}, f32[512,512]{1,0:T(8,128)S(1)}, u32[]{:S(2)}, u32[]{:S(2)}) collective-permute-start(f32[512,512]{1,0:T(8,128)S(1)} %get-tuple-element.13), channel_id=1, source_target_pairs={{0,8},{8,0},{1,9},{9,1},{2,10},{10,2},{3,11},{11,3},{4,12},{12,4},... | collective-permute-start | bytes 3145736 | tf_op jit(solution)/shard_map/ppermute | solution.py:248
  12.0 9.4 %all_to_all.20 = f32[16,1,128]{2,1,0:T(1,128)S(1)} all-to-all(f32[16,1,128]{2,1,0:T(1,128)S(1)} %bitcast.21), channel_id=1, replica_groups=mesh['x'=4,'z'=8,'core'=2,'tensor'=8] {'core','tensor'}, dimensions={0} | all-to-all | bytes 16384 | tf_op jit(solution)/shard_map/all_to_all | solution.py:148
  21.4 20.5 %all_to_all.21 = f32[32,1,128]{2,1,0:T(1,128)S(1)} all-to-all(f32[32,1,128]{2,1,0:T(1,128)S(1)} %bitcast.19), channel_id=1, replica_groups=mesh['x'=4,'z'=8,'core'=2,'tensor'=8] {'x','z'}, dimensions={0} | all-to-all | bytes 32768 | tf_op jit(solution)/shard_map/all_to_all | solution.py:148
  42.0 0.0 collective-permute-done.received
  42.0 0.2 chip_codes.1
  42.2 15.9 %all_to_all.22.refs_1_ = f32[32,8,512]{2,1,0:T(8,128)S(1)} all-to-all(f32[32,8,512]{2,1,0:T(8,128)S(1)} %bitcast.13), channel_id=1, replica_groups=mesh['x'=4,'z'=8,'core'=2,'tensor'=8] {'x','z'}, dimensions={0} | all-to-all | bytes 1048576 | tf_op jit(solution)/shard_map/all_to_all | solution.py:254
  58.1 0.2 owned_mean.1
  58.3 19.7 %all_to_all.23 = f32[32,8,512]{2,1,0:T(8,128)S(1)} all-to-all(f32[32,8,512]{2,1,0:T(8,128)S(1)} %owned_mean.1), channel_id=1, replica_groups=mesh['x'=4,'z'=8,'core'=2,'tensor'=8] {'x','z'}, dimensions={0} | all-to-all | bytes 1048576 | tf_op jit(solution)/shard_map/all_to_all | solution.py:257
  78.0 7.2 %collective-permute-start.1 = (f32[256,512]{1,0:T(8,128)S(1)}, f32[256,512]{1,0:T(8,128)S(1)}, u32[]{:S(2)}, u32[]{:S(2)}) collective-permute-start(f32[256,512]{1,0:T(8,128)S(1)} %bitcast.14), channel_id=1, source_target_pairs={{0,8},{8,0},{1,9},{9,1},{2,10},{10,2},{3,11},{11,3},{4,12},{12,4},... | collective-permute-start | bytes 1572872 | tf_op jit(solution)/shard_map/ppermute | solution.py:259
  85.3 1.3 %store_mine.1 = (f32[512,512]{1,0:T(8,128)}, f32[1,1]{1,0:T(1,128)}) custom-call(f32[256,512]{1,0:T(8,128)S(1)} %bitcast.15, f32[32,128]{1,0:T(8,128)S(1)} %bitcast.18), custom_call_target="tpu_custom_call" | custom-call | tf_op jit(solution)/shard_map/store_mine/pallas_call | solution.py:211
  86.6 0.2 collective-permute-done.1.half
  86.8 0.8 store_other.1
  (1 shorter events, 0.0 us)
Async XLA Ops:
  3.3 38.7 %collective-permute-start = (f32[512,512]{1,0:T(8,128)S(1)}, f32[512,512]{1,0:T(8,128)S(1)}, u32[]{:S(2)}, u32[]{:S(2)}) collective-permute-start(f32[512,512]{1,0:T(8,128)S(1)} %get-tuple-element.13), channel_id=1, source_target_pairs={{0,8},{8,0},{1,9},{9,1},{2,10},{10,2},{3,11},{11,3},{4,12},{12,4},... | collective-permute-start | bytes 3145736 | tf_op jit(solution)/shard_map/ppermute | solution.py:248
  78.0 8.8 %collective-permute-start.1 = (f32[256,512]{1,0:T(8,128)S(1)}, f32[256,512]{1,0:T(8,128)S(1)}, u32[]{:S(2)}, u32[]{:S(2)}) collective-permute-start(f32[256,512]{1,0:T(8,128)S(1)} %bitcast.14), channel_id=1, source_target_pairs={{0,8},{8,0},{1,9},{9,1},{2,10},{10,2},{3,11},{11,3},{4,12},{12,4},... | collective-permute-start | bytes 1572872 | tf_op jit(solution)/shard_map/ppermute | solution.py:259

commit v5 on v4

--- a/solution.py
+++ b/solution.py
@@ -139,6 +139,7 @@
         out_specs=VMEM,
         out_shape=jax.ShapeDtypeStruct((peers, 128), jnp.float32),
         compiler_params=LIMIT,
+        cost_estimate=pl.CostEstimate(flops=3 * 10**10, bytes_accessed=0, transcendentals=0),
         name="highest",
     )(tops)
 
@@ -245,10 +246,9 @@
     own, own_dither, send, tops, matrix, own_signs = rotate(
         grads[0], signs, dither[0], matrix, mean_rows, lax.axis_size(NEAR)
     )
+    tops = exchange(tops, NEAR)
     received = lax.ppermute(send, "core", swap)
-
-    tops = highest(exchange(tops, NEAR), lax.axis_size(FAR))
-    tops = exchange(tops, FAR)
+    tops = exchange(highest(tops, lax.axis_size(FAR)), FAR)
 
     codes = chip_codes(tops, own, own_dither, received)
     codes = lax.all_to_all(codes.reshape(chips, mean_rows, length), CHIPS, 0, 0)

time: 87.9 us -> 86.6 us (0.985)
  blocking collectives: 65.6 us -> 55.4 us
  waiting for transfers between devices: 0.18 us -> 4.95 us
  starting transfers between devices: 16 us -> 19.5 us
    all_to_all x0 -> x1, starting transfers between devices: none -> 10.2 us  [exchange(): lax.all_to_all(tops.reshape(peers, 1, lanes), axes, 0, 0)]
    all_to_all x2 -> x1, blocking collectives: 29.9 us -> 19.8 us  [exchange(): lax.all_to_all(tops.reshape(peers, 1, lanes), axes, 0, 0)]
    ppermute x1, starting transfers between devices: 8.79 us -> 2.08 us  [shards(): received = lax.ppermute(send, 'core', swap)]
    all_to_all x0 -> x1, waiting for transfers between devices: none -> 4.77 us  [exchange(): lax.all_to_all(tops.reshape(peers, 1, lanes), axes, 0, 0)]
  transfers between devices with their start and end apart: 2 -> 3, of which waited for: 1 -> 2; matrix products, arithmetic and copies ran while one was open for 0% -> 0% of each run, Pallas kernels for 2% -> 2%
where the time goes in v5:
time: 86.6 us; the launch traced here: 86.3 us
  blocking collectives  55.4 us (64%)
  starting transfers between devices  19.5 us (23%)
  Pallas kernels  5.76 us (7%)
  waiting for transfers between devices  4.95 us (6%)
    all_to_all x1, blocking collectives, exchange(): lax.all_to_all(tops.reshape(peers, 1, lanes), axes, 0, 0)  19.8 us
    all_to_all x1, blocking collectives, shards(): mean = lax.all_to_all(mean, CHIPS, 0, 0).reshape(rows // 2, length)  19.7 us
    all_to_all x1, blocking collectives, shards(): codes = lax.all_to_all(codes.reshape(chips, mean_rows, length), CHIPS, 0, 0)  15.9 us
    all_to_all x1, starting transfers between devices, exchange(): lax.all_to_all(tops.reshape(peers, 1, lanes), axes, 0, 0)  10.2 us
    ppermute x1, starting transfers between devices, shards(): other = lax.ppermute(mean, 'core', swap)  7.24 us
    all_to_all x1, waiting for transfers between devices, exchange(): lax.all_to_all(tops.reshape(peers, 1, lanes), axes, 0, 0)  4.77 us
    pallas_call x1, Pallas kernels, rotate(): pl.pallas_call(rotate_kernel, in_specs=[HBM] * 4, out_specs=[VMEM] * 6, o...  3.22 us
    ppermute x1, starting transfers between devices, shards(): received = lax.ppermute(send, 'core', swap)  2.08 us
  transfers between devices with their start and end apart: 3, of which 2 were waited for; matrix products, arithmetic and copies ran while one was open for 0% of the time, Pallas kernels for 2%

profile of v5, /device:TPU:1, one launch (start us, length us, event | category | flops | bytes accessed | tf_op | source)
XLA Modules:
  0.0 86.3 jit_solution(10707474035647983267)
XLA Ops:
  0.6 3.2 %rotate.1 = (f32[256,512]{1,0:T(8,128)S(1)}, s32[256,512]{1,0:T(8,128)S(1)}, f32[512,512]{1,0:T(8,128)S(1)}, f32[16,128]{1,0:T(8,128)}, bf16[256,256]{1,0:T(8,128)(2,1)S(1)}, /*index=5*/f32[8,512]{1,0:T(8,128)S(1)}) custom-call(f32[512,512]{1,0:T(8,128)} %bitcast.21, s32[512,512]{1,0:T(8,128)} %signs.1, s32[512,512]{1,0:T(8,128)} %bitcast.22, ...), custom_call_target="tpu_custom_call" | custom-call | tf_op jit(solution)/shard_map/rotate/pallas_call | solution.py:107
  3.9 10.2 %all-to-all-start = ((f32[16,1,128]{2,1,0:T(1,128)}), f32[16,1,128]{2,1,0:T(1,128)S(1)}, u32[]{:S(2)}, u32[]{:S(2)}) async-start(f32[16,1,128]{2,1,0:T(1,128)} %bitcast.3), calls=%async_computation | async-start | bytes 16384 | tf_op jit(solution)/shard_map/all_to_all | solution.py:149
  14.1 2.1 %collective-permute-start = (f32[512,512]{1,0:T(8,128)S(1)}, f32[512,512]{1,0:T(8,128)S(1)}, u32[]{:S(2)}, u32[]{:S(2)}) collective-permute-start(f32[512,512]{1,0:T(8,128)S(1)} %get-tuple-element.13), channel_id=1, source_target_pairs={{0,8},{8,0},{1,9},{9,1},{2,10},{10,2},{3,11},{11,3},{4,12},{12,4},... | collective-permute-start | bytes 3145736 | tf_op jit(solution)/shard_map/ppermute | solution.py:250
  16.1 4.8 %all-to-all-done = f32[16,1,128]{2,1,0:T(1,128)S(1)} async-done(((f32[16,1,128]{2,1,0:T(1,128)}), f32[16,1,128]{2,1,0:T(1,128)S(1)}, u32[]{:S(2)}, u32[]{:S(2)}) %all-to-all-start) | async-done | bytes 8224 | tf_op jit(solution)/shard_map/all_to_all | solution.py:149
  20.9 19.8 %all_to_all.20 = f32[32,1,128]{2,1,0:T(1,128)S(1)} all-to-all(f32[32,1,128]{2,1,0:T(1,128)S(1)} %bitcast.19), channel_id=1, replica_groups=mesh['x'=4,'z'=8,'core'=2,'tensor'=8] {'x','z'}, dimensions={0} | all-to-all | bytes 32768 | tf_op jit(solution)/shard_map/all_to_all | solution.py:149
  40.7 0.0 collective-permute-done.received
  40.7 0.2 chip_codes.1
  40.9 15.9 %all_to_all.21.refs_1_ = f32[32,8,512]{2,1,0:T(8,128)S(1)} all-to-all(f32[32,8,512]{2,1,0:T(8,128)S(1)} %bitcast.13), channel_id=1, replica_groups=mesh['x'=4,'z'=8,'core'=2,'tensor'=8] {'x','z'}, dimensions={0} | all-to-all | bytes 1048576 | tf_op jit(solution)/shard_map/all_to_all | solution.py:254
  56.8 0.2 owned_mean.1
  57.1 19.7 %all_to_all.22 = f32[32,8,512]{2,1,0:T(8,128)S(1)} all-to-all(f32[32,8,512]{2,1,0:T(8,128)S(1)} %owned_mean.1), channel_id=1, replica_groups=mesh['x'=4,'z'=8,'core'=2,'tensor'=8] {'x','z'}, dimensions={0} | all-to-all | bytes 1048576 | tf_op jit(solution)/shard_map/all_to_all | solution.py:257
  76.8 7.2 %collective-permute-start.1 = (f32[256,512]{1,0:T(8,128)S(1)}, f32[256,512]{1,0:T(8,128)S(1)}, u32[]{:S(2)}, u32[]{:S(2)}) collective-permute-start(f32[256,512]{1,0:T(8,128)S(1)} %bitcast.14), channel_id=1, source_target_pairs={{0,8},{8,0},{1,9},{9,1},{2,10},{10,2},{3,11},{11,3},{4,12},{12,4},... | collective-permute-start | bytes 1572872 | tf_op jit(solution)/shard_map/ppermute | solution.py:259
  84.0 1.3 %store_mine.1 = (f32[512,512]{1,0:T(8,128)}, f32[1,1]{1,0:T(1,128)}) custom-call(f32[256,512]{1,0:T(8,128)S(1)} %bitcast.15, f32[32,128]{1,0:T(8,128)S(1)} %bitcast.18), custom_call_target="tpu_custom_call" | custom-call | tf_op jit(solution)/shard_map/store_mine/pallas_call | solution.py:212
  85.3 0.2 collective-permute-done.1.half
  85.5 0.8 store_other.1
  (1 shorter events, 0.0 us)
Async XLA Ops:
  3.9 17.1 %all-to-all-start = ((f32[16,1,128]{2,1,0:T(1,128)}), f32[16,1,128]{2,1,0:T(1,128)S(1)}, u32[]{:S(2)}, u32[]{:S(2)}) async-start(f32[16,1,128]{2,1,0:T(1,128)} %bitcast.3), calls=%async_computation | async-start | bytes 16384 | tf_op jit(solution)/shard_map/all_to_all | solution.py:149
  14.1 26.7 %collective-permute-start = (f32[512,512]{1,0:T(8,128)S(1)}, f32[512,512]{1,0:T(8,128)S(1)}, u32[]{:S(2)}, u32[]{:S(2)}) collective-permute-start(f32[512,512]{1,0:T(8,128)S(1)} %get-tuple-element.13), channel_id=1, source_target_pairs={{0,8},{8,0},{1,9},{9,1},{2,10},{10,2},{3,11},{11,3},{4,12},{12,4},... | collective-permute-start | bytes 3145736 | tf_op jit(solution)/shard_map/ppermute | solution.py:250
  76.8 8.8 %collective-permute-start.1 = (f32[256,512]{1,0:T(8,128)S(1)}, f32[256,512]{1,0:T(8,128)S(1)}, u32[]{:S(2)}, u32[]{:S(2)}) collective-permute-start(f32[256,512]{1,0:T(8,128)S(1)} %bitcast.14), channel_id=1, source_target_pairs={{0,8},{8,0},{1,9},{9,1},{2,10},{10,2},{3,11},{11,3},{4,12},{12,4},... | collective-permute-start | bytes 1572872 | tf_op jit(solution)/shard_map/ppermute | solution.py:259

commit v6 on v5

--- a/solution.py
+++ b/solution.py
@@ -12,6 +12,7 @@
 CHIPS = ("x", "z")
 NEAR, FAR = ("core", "tensor"), ("x", "z")
 STRIPE = 64
+FIRST = {"x": 2, "z": 5, "tensor": 4}
 
 
 def signs_matrix(length):
@@ -45,6 +46,11 @@
         out = out + products[2 * rows * i : 2 * rows * (i + 1)]
     out = out * (1.0 / math.sqrt(length))
     return jnp.concatenate([out[:rows], out[rows:]], axis=1)
+
+
+def counted(axis):
+    size = lax.axis_size(axis)
+    return lax.rem(lax.axis_index(axis) + (size - FIRST[axis] % size), size)
 
 
 def rotate_kernel(
@@ -89,7 +95,7 @@
     get_others.wait()
     send[high, :] = dither_buf[...].astype(jnp.float32)
     mean_rows = own_signs.shape[0]
-    chip = lax.axis_index("x") * lax.axis_size("z") + lax.axis_index("z")
+    chip = counted("x") * lax.axis_size("z") + counted("z")
     here = pl.ds(pl.multiple_of(half + chip * mean_rows, mean_rows), mean_rows)
     own_signs[...] = signs_buf[here, :].astype(jnp.float32)
     get_mine.wait()
@@ -144,9 +150,18 @@
     )(tops)
 
 
+def all_to_all(values, axes):
+    sizes = [lax.axis_size(axis) for axis in axes]
+    peers = np.arange(math.prod(sizes)).reshape(sizes)
+    for dim, axis in enumerate(axes):
+        peers = np.roll(peers, -FIRST.get(axis, 0), dim)
+    group = [int(peer) for peer in peers.reshape(-1)]
+    return lax.all_to_all(values, axes, 0, 0, axis_index_groups=[group])
+
+
 def exchange(tops, axes):
     peers, lanes = tops.shape
-    return lax.all_to_all(tops.reshape(peers, 1, lanes), axes, 0, 0).reshape(peers, lanes)
+    return all_to_all(tops.reshape(peers, 1, lanes), axes).reshape(peers, lanes)
 
 
 def codes_kernel(tops, own, dither, received, codes):
@@ -251,10 +266,10 @@
     tops = exchange(highest(tops, lax.axis_size(FAR)), FAR)
 
     codes = chip_codes(tops, own, own_dither, received)
-    codes = lax.all_to_all(codes.reshape(chips, mean_rows, length), CHIPS, 0, 0)
+    codes = all_to_all(codes.reshape(chips, mean_rows, length), CHIPS)
 
     mean = owned_mean(CORES * chips, tops, codes, own_signs, matrix)
-    mean = lax.all_to_all(mean, CHIPS, 0, 0).reshape(rows // 2, length)
+    mean = all_to_all(mean, CHIPS).reshape(rows // 2, length)
 
     other = lax.ppermute(mean, "core", swap)
     mean_grad, quant_step = store_mine(mean, tops)

time: 86.6 us -> 82.4 us (0.952)
  waiting for transfers between devices: 4.95 us -> 0.18 us
    all_to_all x1, waiting for transfers between devices: 4.77 us -> 0.01 us  [all_to_all(): return lax.all_to_all(values, axes, 0, 0, axis_index_groups=[group])]
    all_to_all x1, starting transfers between devices: 10.2 us -> 13.8 us  [all_to_all(): return lax.all_to_all(values, axes, 0, 0, axis_index_groups=[group])]
    ppermute x1, starting transfers between devices: 7.24 us -> 4.31 us  [shards(): other = lax.ppermute(mean, 'core', swap)]
  transfers between devices with their start and end apart: 3 -> 3, of which waited for: 2 -> 1; matrix products, arithmetic and copies ran while one was open for 0% -> 0% of each run, Pallas kernels for 2% -> 2%
where the time goes in v6:
time: 82.4 us; the launch traced here: 82.1 us
  blocking collectives  55.2 us (67%)
  starting transfers between devices  20.3 us (25%)
  Pallas kernels  5.76 us (7%)
    all_to_all x3, blocking collectives, all_to_all(): return lax.all_to_all(values, axes, 0, 0, axis_index_groups=[group])  55.2 us
    all_to_all x1, starting transfers between devices, all_to_all(): return lax.all_to_all(values, axes, 0, 0, axis_index_groups=[group])  13.8 us
    ppermute x1, starting transfers between devices, shards(): other = lax.ppermute(mean, 'core', swap)  4.31 us
    pallas_call x1, Pallas kernels, rotate(): pl.pallas_call(rotate_kernel, in_specs=[HBM] * 4, out_specs=[VMEM] * 6, o...  3.22 us
    ppermute x1, starting transfers between devices, shards(): received = lax.ppermute(send, 'core', swap)  2.26 us
  transfers between devices with their start and end apart: 3, of which 1 were waited for; matrix products, arithmetic and copies ran while one was open for 0% of the time, Pallas kernels for 2%

profile of v6, /device:TPU:1, one launch (start us, length us, event | category | flops | bytes accessed | tf_op | source)
XLA Modules:
  0.0 82.1 jit_solution(3955052243211749336)
XLA Ops:
  0.6 3.2 %rotate.1 = (f32[256,512]{1,0:T(8,128)S(1)}, s32[256,512]{1,0:T(8,128)S(1)}, f32[512,512]{1,0:T(8,128)S(1)}, f32[16,128]{1,0:T(8,128)}, bf16[256,256]{1,0:T(8,128)(2,1)S(1)}, /*index=5*/f32[8,512]{1,0:T(8,128)S(1)}) custom-call(f32[512,512]{1,0:T(8,128)} %bitcast.21, s32[512,512]{1,0:T(8,128)} %signs.1, s32[512,512]{1,0:T(8,128)} %bitcast.22, ...), custom_call_target="tpu_custom_call" | custom-call | tf_op jit(solution)/shard_map/rotate/pallas_call | solution.py:113
  3.9 13.8 %all-to-all-start = ((f32[16,1,128]{2,1,0:T(1,128)}), f32[16,1,128]{2,1,0:T(1,128)S(1)}, u32[]{:S(2)}, u32[]{:S(2)}) async-start(f32[16,1,128]{2,1,0:T(1,128)} %bitcast.3), calls=%async_computation | async-start | bytes 16384 | tf_op jit(solution)/shard_map/all_to_all | solution.py:159
  17.6 2.3 %collective-permute-start = (f32[512,512]{1,0:T(8,128)S(1)}, f32[512,512]{1,0:T(8,128)S(1)}, u32[]{:S(2)}, u32[]{:S(2)}) collective-permute-start(f32[512,512]{1,0:T(8,128)S(1)} %get-tuple-element.13), channel_id=1, source_target_pairs={{0,8},{8,0},{1,9},{9,1},{2,10},{10,2},{3,11},{11,3},{4,12},{12,4},... | collective-permute-start | bytes 3145736 | tf_op jit(solution)/shard_map/ppermute | solution.py:265
  19.9 0.0 all-to-all-done
  19.9 14.0 %all_to_all.20 = f32[32,1,128]{2,1,0:T(1,128)S(1)} all-to-all(f32[32,1,128]{2,1,0:T(1,128)S(1)} %bitcast.19), channel_id=1, replica_groups={{336,352,368,256,272,288,304,320,464,480,496,384,400,416,432,448,80,96,..., dimensions={0} | all-to-all | bytes 32768 | tf_op jit(solution)/shard_map/all_to_all | solution.py:159
  33.9 0.0 collective-permute-done.received
  33.9 0.2 chip_codes.1
  34.1 20.3 %all_to_all.21.refs_1_ = f32[32,8,512]{2,1,0:T(8,128)S(1)} all-to-all(f32[32,8,512]{2,1,0:T(8,128)S(1)} %bitcast.13), channel_id=1, replica_groups={{336,352,368,256,272,288,304,320,464,480,496,384,400,416,432,448,80,96,..., dimensions={0} | all-to-all | bytes 1048576 | tf_op jit(solution)/shard_map/all_to_all | solution.py:159
  54.4 0.2 owned_mean.1
  54.6 20.9 %all_to_all.22 = f32[32,8,512]{2,1,0:T(8,128)S(1)} all-to-all(f32[32,8,512]{2,1,0:T(8,128)S(1)} %owned_mean.1), channel_id=1, replica_groups={{336,352,368,256,272,288,304,320,464,480,496,384,400,416,432,448,80,96,..., dimensions={0} | all-to-all | bytes 1048576 | tf_op jit(solution)/shard_map/all_to_all | solution.py:159
  75.5 4.3 %collective-permute-start.1 = (f32[256,512]{1,0:T(8,128)S(1)}, f32[256,512]{1,0:T(8,128)S(1)}, u32[]{:S(2)}, u32[]{:S(2)}) collective-permute-start(f32[256,512]{1,0:T(8,128)S(1)} %bitcast.14), channel_id=1, source_target_pairs={{0,8},{8,0},{1,9},{9,1},{2,10},{10,2},{3,11},{11,3},{4,12},{12,4},... | collective-permute-start | bytes 1572872 | tf_op jit(solution)/shard_map/ppermute | solution.py:274
  79.8 1.3 %store_mine.1 = (f32[512,512]{1,0:T(8,128)}, f32[1,1]{1,0:T(1,128)}) custom-call(f32[256,512]{1,0:T(8,128)S(1)} %bitcast.15, f32[32,128]{1,0:T(8,128)S(1)} %bitcast.18), custom_call_target="tpu_custom_call" | custom-call | tf_op jit(solution)/shard_map/store_mine/pallas_call | solution.py:227
  81.2 0.2 collective-permute-done.1.half
  81.3 0.8 store_other.1
  (1 shorter events, 0.0 us)
Async XLA Ops:
  3.9 16.0 %all-to-all-start = ((f32[16,1,128]{2,1,0:T(1,128)}), f32[16,1,128]{2,1,0:T(1,128)S(1)}, u32[]{:S(2)}, u32[]{:S(2)}) async-start(f32[16,1,128]{2,1,0:T(1,128)} %bitcast.3), calls=%async_computation | async-start | bytes 16384 | tf_op jit(solution)/shard_map/all_to_all | solution.py:159
  17.6 16.3 %collective-permute-start = (f32[512,512]{1,0:T(8,128)S(1)}, f32[512,512]{1,0:T(8,128)S(1)}, u32[]{:S(2)}, u32[]{:S(2)}) collective-permute-start(f32[512,512]{1,0:T(8,128)S(1)} %get-tuple-element.13), channel_id=1, source_target_pairs={{0,8},{8,0},{1,9},{9,1},{2,10},{10,2},{3,11},{11,3},{4,12},{12,4},... | collective-permute-start | bytes 3145736 | tf_op jit(solution)/shard_map/ppermute | solution.py:265
  75.5 5.8 %collective-permute-start.1 = (f32[256,512]{1,0:T(8,128)S(1)}, f32[256,512]{1,0:T(8,128)S(1)}, u32[]{:S(2)}, u32[]{:S(2)}) collective-permute-start(f32[256,512]{1,0:T(8,128)S(1)} %bitcast.14), channel_id=1, source_target_pairs={{0,8},{8,0},{1,9},{9,1},{2,10},{10,2},{3,11},{11,3},{4,12},{12,4},... | collective-permute-start | bytes 1572872 | tf_op jit(solution)/shard_map/ppermute | solution.py:274

commit v7 on v6

--- a/solution.py
+++ b/solution.py
@@ -10,7 +10,7 @@
 
 Z, CORES = 8, 2
 CHIPS = ("x", "z")
-NEAR, FAR = ("core", "tensor"), ("x", "z")
+NEAR, FAR = ("core", "z"), ("x", "tensor")
 STRIPE = 64
 FIRST = {"x": 2, "z": 5, "tensor": 4}
 

time: 82.4 us -> 81.4 us (0.988)
  blocking collectives: 55.2 us -> 53.5 us
    all_to_all x3, blocking collectives: 55.2 us -> 53.5 us  [all_to_all(): return lax.all_to_all(values, axes, 0, 0, axis_index_groups=[group])]
  transfers between devices with their start and end apart: 3 -> 3, of which waited for: 1 -> 2; matrix products, arithmetic and copies ran while one was open for 0% -> 0% of each run, Pallas kernels for 2% -> 2%
where the time goes in v7:
time: 81.4 us; the launch traced here: 81.1 us
  blocking collectives  53.5 us (66%)
  starting transfers between devices  20.4 us (25%)
  Pallas kernels  5.76 us (7%)
    all_to_all x3, blocking collectives, all_to_all(): return lax.all_to_all(values, axes, 0, 0, axis_index_groups=[group])  53.5 us
    all_to_all x1, starting transfers between devices, all_to_all(): return lax.all_to_all(values, axes, 0, 0, axis_index_groups=[group])  13.8 us
    ppermute x1, starting transfers between devices, shards(): other = lax.ppermute(mean, 'core', swap)  4.28 us
    pallas_call x1, Pallas kernels, rotate(): pl.pallas_call(rotate_kernel, in_specs=[HBM] * 4, out_specs=[VMEM] * 6, o...  3.22 us
    ppermute x1, starting transfers between devices, shards(): received = lax.ppermute(send, 'core', swap)  2.26 us
  transfers between devices with their start and end apart: 3, of which 2 were waited for; matrix products, arithmetic and copies ran while one was open for 0% of the time, Pallas kernels for 2%

profile of v7, /device:TPU:1, one launch (start us, length us, event | category | flops | bytes accessed | tf_op | source)
XLA Modules:
  0.0 81.1 jit_solution(1386915709896437938)
XLA Ops:
  0.6 3.2 %rotate.1 = (f32[256,512]{1,0:T(8,128)S(1)}, s32[256,512]{1,0:T(8,128)S(1)}, f32[512,512]{1,0:T(8,128)S(1)}, f32[16,128]{1,0:T(8,128)}, bf16[256,256]{1,0:T(8,128)(2,1)S(1)}, /*index=5*/f32[8,512]{1,0:T(8,128)S(1)}) custom-call(f32[512,512]{1,0:T(8,128)} %bitcast.21, s32[512,512]{1,0:T(8,128)} %signs.1, s32[512,512]{1,0:T(8,128)} %bitcast.22, ...), custom_call_target="tpu_custom_call" | custom-call | tf_op jit(solution)/shard_map/rotate/pallas_call | solution.py:113
  3.9 13.8 %all-to-all-start = ((f32[16,1,128]{2,1,0:T(1,128)}), f32[16,1,128]{2,1,0:T(1,128)S(1)}, u32[]{:S(2)}, u32[]{:S(2)}) async-start(f32[16,1,128]{2,1,0:T(1,128)} %bitcast.3), calls=%async_computation | async-start | bytes 16384 | tf_op jit(solution)/shard_map/all_to_all | solution.py:159
  17.7 2.3 %collective-permute-start = (f32[512,512]{1,0:T(8,128)S(1)}, f32[512,512]{1,0:T(8,128)S(1)}, u32[]{:S(2)}, u32[]{:S(2)}) collective-permute-start(f32[512,512]{1,0:T(8,128)S(1)} %get-tuple-element.13), channel_id=1, source_target_pairs={{0,8},{8,0},{1,9},{9,1},{2,10},{10,2},{3,11},{11,3},{4,12},{12,4},... | collective-permute-start | bytes 3145736 | tf_op jit(solution)/shard_map/ppermute | solution.py:265
  20.0 0.6 all-to-all-done
  20.6 12.2 %all_to_all.20 = f32[32,1,128]{2,1,0:T(1,128)S(1)} all-to-all(f32[32,1,128]{2,1,0:T(1,128)S(1)} %bitcast.19), channel_id=1, replica_groups={{260,261,262,263,256,257,258,259,388,389,390,391,384,385,386,387,4,5,6,..., dimensions={0} | all-to-all | bytes 32768 | tf_op jit(solution)/shard_map/all_to_all | solution.py:159
  32.7 0.0 collective-permute-done.received
  32.7 0.2 chip_codes.1
  32.9 20.2 %all_to_all.21.refs_1_ = f32[32,8,512]{2,1,0:T(8,128)S(1)} all-to-all(f32[32,8,512]{2,1,0:T(8,128)S(1)} %bitcast.13), channel_id=1, replica_groups={{336,352,368,256,272,288,304,320,464,480,496,384,400,416,432,448,80,96,..., dimensions={0} | all-to-all | bytes 1048576 | tf_op jit(solution)/shard_map/all_to_all | solution.py:159
  53.1 0.2 owned_mean.1
  53.4 21.1 %all_to_all.22 = f32[32,8,512]{2,1,0:T(8,128)S(1)} all-to-all(f32[32,8,512]{2,1,0:T(8,128)S(1)} %owned_mean.1), channel_id=1, replica_groups={{336,352,368,256,272,288,304,320,464,480,496,384,400,416,432,448,80,96,..., dimensions={0} | all-to-all | bytes 1048576 | tf_op jit(solution)/shard_map/all_to_all | solution.py:159
  74.5 4.3 %collective-permute-start.1 = (f32[256,512]{1,0:T(8,128)S(1)}, f32[256,512]{1,0:T(8,128)S(1)}, u32[]{:S(2)}, u32[]{:S(2)}) collective-permute-start(f32[256,512]{1,0:T(8,128)S(1)} %bitcast.14), channel_id=1, source_target_pairs={{0,8},{8,0},{1,9},{9,1},{2,10},{10,2},{3,11},{11,3},{4,12},{12,4},... | collective-permute-start | bytes 1572872 | tf_op jit(solution)/shard_map/ppermute | solution.py:274
  78.7 1.3 %store_mine.1 = (f32[512,512]{1,0:T(8,128)}, f32[1,1]{1,0:T(1,128)}) custom-call(f32[256,512]{1,0:T(8,128)S(1)} %bitcast.15, f32[32,128]{1,0:T(8,128)S(1)} %bitcast.18), custom_call_target="tpu_custom_call" | custom-call | tf_op jit(solution)/shard_map/store_mine/pallas_call | solution.py:227
  80.1 0.2 collective-permute-done.1.half
  80.3 0.8 store_other.1
  (1 shorter events, 0.0 us)
Async XLA Ops:
  3.9 16.7 %all-to-all-start = ((f32[16,1,128]{2,1,0:T(1,128)}), f32[16,1,128]{2,1,0:T(1,128)S(1)}, u32[]{:S(2)}, u32[]{:S(2)}) async-start(f32[16,1,128]{2,1,0:T(1,128)} %bitcast.3), calls=%async_computation | async-start | bytes 16384 | tf_op jit(solution)/shard_map/all_to_all | solution.py:159
  17.7 15.0 %collective-permute-start = (f32[512,512]{1,0:T(8,128)S(1)}, f32[512,512]{1,0:T(8,128)S(1)}, u32[]{:S(2)}, u32[]{:S(2)}) collective-permute-start(f32[512,512]{1,0:T(8,128)S(1)} %get-tuple-element.13), channel_id=1, source_target_pairs={{0,8},{8,0},{1,9},{9,1},{2,10},{10,2},{3,11},{11,3},{4,12},{12,4},... | collective-permute-start | bytes 3145736 | tf_op jit(solution)/shard_map/ppermute | solution.py:265
  74.5 5.8 %collective-permute-start.1 = (f32[256,512]{1,0:T(8,128)S(1)}, f32[256,512]{1,0:T(8,128)S(1)}, u32[]{:S(2)}, u32[]{:S(2)}) collective-permute-start(f32[256,512]{1,0:T(8,128)S(1)} %bitcast.14), channel_id=1, source_target_pairs={{0,8},{8,0},{1,9},{9,1},{2,10},{10,2},{3,11},{11,3},{4,12},{12,4},... | collective-permute-start | bytes 1572872 | tf_op jit(solution)/shard_map/ppermute | solution.py:274

commit v8 on v7

--- a/solution.py
+++ b/solution.py
@@ -55,7 +55,7 @@
 
 def rotate_kernel(
     grads, signs, dither, matrix_in, own, own_dither, send, tops, matrix, own_signs,
-    grads_buf, signs_buf, dither_buf, fetched, kept,
+    grads_buf, signs_buf, dither_buf, tops_buf, fetched, kept,
 ):
     rows, length = grads.shape
     half = rows // 2
@@ -91,7 +91,9 @@
         rotated = transform(grads_buf[place, :] * signs_buf[place, :].astype(jnp.float32), matrix[...], 3)
         top = jnp.maximum(top, jnp.max(jnp.abs(rotated).reshape(half // 8, 8, length), axis=0))
         result[low, :] = rotated
-    tops[...] = jnp.full(tops.shape, jnp.max(top), jnp.float32)
+    tops_buf[...] = jnp.full(tops.shape, jnp.max(top), jnp.float32)
+    put_tops = pltpu.make_async_copy(tops_buf, tops, kept.at[3])
+    put_tops.start()
     get_others.wait()
     send[high, :] = dither_buf[...].astype(jnp.float32)
     mean_rows = own_signs.shape[0]
@@ -99,6 +101,7 @@
     here = pl.ds(pl.multiple_of(half + chip * mean_rows, mean_rows), mean_rows)
     own_signs[...] = signs_buf[here, :].astype(jnp.float32)
     get_mine.wait()
+    put_tops.wait()
 
 
 VMEM = pl.BlockSpec(memory_space=pltpu.VMEM)
@@ -113,7 +116,7 @@
     return pl.pallas_call(
         rotate_kernel,
         in_specs=[HBM] * 4,
-        out_specs=[VMEM] * 6,
+        out_specs=[VMEM, VMEM, VMEM, HBM, VMEM, VMEM],
         out_shape=[
             jax.ShapeDtypeStruct((half, length), jnp.float32),
             jax.ShapeDtypeStruct((half, length), jnp.int32),
@@ -126,8 +129,9 @@
             pltpu.VMEM((rows, length), jnp.float32),
             pltpu.VMEM((rows, length), jnp.int32),
             pltpu.VMEM((half, length), jnp.int32),
+            pltpu.VMEM((peers, 128), jnp.float32),
             pltpu.SemaphoreType.DMA((2, 2)),
-            pltpu.SemaphoreType.DMA((3,)),
+            pltpu.SemaphoreType.DMA((4,)),
         ],
         compiler_params=LIMIT,
         name="rotate",

time: 81.4 us -> 81.4 us (level)
  no operation moved by 1% of the time
where the time goes in v8:
time: 81.4 us; the launch traced here: 81 us
  blocking collectives  53.5 us (66%)
  starting transfers between devices  20.4 us (25%)
  Pallas kernels  5.72 us (7%)
    all_to_all x3, blocking collectives, all_to_all(): return lax.all_to_all(values, axes, 0, 0, axis_index_groups=[group])  53.5 us
    all_to_all x1, starting transfers between devices, all_to_all(): return lax.all_to_all(values, axes, 0, 0, axis_index_groups=[group])  13.8 us
    ppermute x1, starting transfers between devices, shards(): other = lax.ppermute(mean, 'core', swap)  4.28 us
    pallas_call x1, Pallas kernels, rotate(): pl.pallas_call(rotate_kernel, in_specs=[HBM] * 4, out_specs=[VMEM, VMEM,...  3.18 us
    ppermute x1, starting transfers between devices, shards(): received = lax.ppermute(send, 'core', swap)  2.26 us
  transfers between devices with their start and end apart: 3, of which 2 were waited for; matrix products, arithmetic and copies ran while one was open for 0% of the time, Pallas kernels for 2%

profile of v8, /device:TPU:1, one launch (start us, length us, event | category | flops | bytes accessed | tf_op | source)
XLA Modules:
  0.0 81.0 jit_solution(694823618916280754)
XLA Ops:
  0.6 3.2 %rotate.1 = (f32[256,512]{1,0:T(8,128)S(1)}, s32[256,512]{1,0:T(8,128)S(1)}, f32[512,512]{1,0:T(8,128)S(1)}, f32[16,128]{1,0:T(8,128)}, bf16[256,256]{1,0:T(8,128)(2,1)S(1)}, /*index=5*/f32[8,512]{1,0:T(8,128)S(1)}) custom-call(f32[512,512]{1,0:T(8,128)} %bitcast.21, s32[512,512]{1,0:T(8,128)} %signs.1, s32[512,512]{1,0:T(8,128)} %bitcast.22, ...), custom_call_target="tpu_custom_call" | custom-call | tf_op jit(solution)/shard_map/rotate/pallas_call | solution.py:116
  3.8 13.8 %all-to-all-start = ((f32[16,1,128]{2,1,0:T(1,128)}), f32[16,1,128]{2,1,0:T(1,128)S(1)}, u32[]{:S(2)}, u32[]{:S(2)}) async-start(f32[16,1,128]{2,1,0:T(1,128)} %bitcast.3), calls=%async_computation | async-start | bytes 16384 | tf_op jit(solution)/shard_map/all_to_all | solution.py:163
  17.7 2.3 %collective-permute-start = (f32[512,512]{1,0:T(8,128)S(1)}, f32[512,512]{1,0:T(8,128)S(1)}, u32[]{:S(2)}, u32[]{:S(2)}) collective-permute-start(f32[512,512]{1,0:T(8,128)S(1)} %get-tuple-element.13), channel_id=1, source_target_pairs={{0,8},{8,0},{1,9},{9,1},{2,10},{10,2},{3,11},{11,3},{4,12},{12,4},... | collective-permute-start | bytes 3145736 | tf_op jit(solution)/shard_map/ppermute | solution.py:269
  19.9 0.6 all-to-all-done
  20.5 12.2 %all_to_all.20 = f32[32,1,128]{2,1,0:T(1,128)S(1)} all-to-all(f32[32,1,128]{2,1,0:T(1,128)S(1)} %bitcast.19), channel_id=1, replica_groups={{260,261,262,263,256,257,258,259,388,389,390,391,384,385,386,387,4,5,6,..., dimensions={0} | all-to-all | bytes 32768 | tf_op jit(solution)/shard_map/all_to_all | solution.py:163
  32.7 0.0 collective-permute-done.received
  32.7 0.2 chip_codes.1
  32.9 20.2 %all_to_all.21.refs_1_ = f32[32,8,512]{2,1,0:T(8,128)S(1)} all-to-all(f32[32,8,512]{2,1,0:T(8,128)S(1)} %bitcast.13), channel_id=1, replica_groups={{336,352,368,256,272,288,304,320,464,480,496,384,400,416,432,448,80,96,..., dimensions={0} | all-to-all | bytes 1048576 | tf_op jit(solution)/shard_map/all_to_all | solution.py:163
  53.1 0.2 owned_mean.1
  53.3 21.1 %all_to_all.22 = f32[32,8,512]{2,1,0:T(8,128)S(1)} all-to-all(f32[32,8,512]{2,1,0:T(8,128)S(1)} %owned_mean.1), channel_id=1, replica_groups={{336,352,368,256,272,288,304,320,464,480,496,384,400,416,432,448,80,96,..., dimensions={0} | all-to-all | bytes 1048576 | tf_op jit(solution)/shard_map/all_to_all | solution.py:163
  74.4 4.3 %collective-permute-start.1 = (f32[256,512]{1,0:T(8,128)S(1)}, f32[256,512]{1,0:T(8,128)S(1)}, u32[]{:S(2)}, u32[]{:S(2)}) collective-permute-start(f32[256,512]{1,0:T(8,128)S(1)} %bitcast.14), channel_id=1, source_target_pairs={{0,8},{8,0},{1,9},{9,1},{2,10},{10,2},{3,11},{11,3},{4,12},{12,4},... | collective-permute-start | bytes 1572872 | tf_op jit(solution)/shard_map/ppermute | solution.py:278
  78.7 1.3 %store_mine.1 = (f32[512,512]{1,0:T(8,128)}, f32[1,1]{1,0:T(1,128)}) custom-call(f32[256,512]{1,0:T(8,128)S(1)} %bitcast.15, f32[32,128]{1,0:T(8,128)S(1)} %bitcast.18), custom_call_target="tpu_custom_call" | custom-call | tf_op jit(solution)/shard_map/store_mine/pallas_call | solution.py:231
  80.0 0.2 collective-permute-done.1.half
  80.2 0.8 store_other.1
  (1 shorter events, 0.0 us)
Async XLA Ops:
  3.8 16.7 %all-to-all-start = ((f32[16,1,128]{2,1,0:T(1,128)}), f32[16,1,128]{2,1,0:T(1,128)S(1)}, u32[]{:S(2)}, u32[]{:S(2)}) async-start(f32[16,1,128]{2,1,0:T(1,128)} %bitcast.3), calls=%async_computation | async-start | bytes 16384 | tf_op jit(solution)/shard_map/all_to_all | solution.py:163
  17.7 15.0 %collective-permute-start = (f32[512,512]{1,0:T(8,128)S(1)}, f32[512,512]{1,0:T(8,128)S(1)}, u32[]{:S(2)}, u32[]{:S(2)}) collective-permute-start(f32[512,512]{1,0:T(8,128)S(1)} %get-tuple-element.13), channel_id=1, source_target_pairs={{0,8},{8,0},{1,9},{9,1},{2,10},{10,2},{3,11},{11,3},{4,12},{12,4},... | collective-permute-start | bytes 3145736 | tf_op jit(solution)/shard_map/ppermute | solution.py:269
  74.4 5.8 %collective-permute-start.1 = (f32[256,512]{1,0:T(8,128)S(1)}, f32[256,512]{1,0:T(8,128)S(1)}, u32[]{:S(2)}, u32[]{:S(2)}) collective-permute-start(f32[256,512]{1,0:T(8,128)S(1)} %bitcast.14), channel_id=1, source_target_pairs={{0,8},{8,0},{1,9},{9,1},{2,10},{10,2},{3,11},{11,3},{4,12},{12,4},... | collective-permute-start | bytes 1572872 | tf_op jit(solution)/shard_map/ppermute | solution.py:278
